TPU v7x, 256 devices: a whole 4x4x8 slice. The times are simulated.
256 devices in a mesh: gx: 4 (over y_hi, core), gy: 8 (over z), gz: 8 (over y_lo, x).
Axes of the slice: x: 4, y: 4 (y_hi: 2, y_lo: 2; y = y_hi * 2 + y_lo), z: 8, core: 2. Of those that a mesh axis runs over, the one named last changes fastest.
Arguments:
- grad_out: bfloat16 [1024, 16384], P(('gx', 'gy'), 'gz'), may hold values from -1.1953125 to 1.1953125
- grad_side: bfloat16 [1024, 16384], P(('gx', 'gy'), 'gz'), may hold values from -1.1953125 to 1.1953125
- attn_out: bfloat16 [1024, 8192], P(('gx', 'gz'), 'gy'), may hold values from -1.796875 to 1.796875
- gate_pre: bfloat16 [1024, 26624], P(('gx', 'gz'), 'gy'), may hold values from -6 to 6
- up_pre: bfloat16 [1024, 26624], P(('gx', 'gz'), 'gy'), may hold values from -6 to 6
- seg_ids: int32 [1024], replicated, may hold values from 0 to 7, never falling along the last dimension, each value on 1 to 256 neighbouring positions
- down_weight: bfloat16 [26624, 16384], P(('gy', 'gx'), 'gz'), may hold values from -0.0390625 to 0.0390625
- out_weight: bfloat16 [8192, 16384], P(('gy', 'gx'), 'gz'), may hold values from -0.0625 to 0.0625
Outputs:
- grad_gate: bfloat16 [1024, 26624], P(('gx', 'gz'), 'gy')
- grad_up: bfloat16 [1024, 26624], P(('gx', 'gz'), 'gy')
- grad_attn: bfloat16 [1024, 8192], P(('gx', 'gz'), 'gy')
- grad_down: bfloat16 [26624, 16384], P(('gy', 'gx'), 'gz')
- grad_outproj: bfloat16 [8192, 16384], P(('gy', 'gx'), 'gz')
Inputs may be any that keep to these rules, and one draw needn't show every extreme that they name: `seg_ids`: each of 8 documents covers 1 to 256 consecutive tokens, ids never fall, and one document has exactly 256 tokens.
All inputs are finite; a program needn't handle non-finite values.
Results may differ from a plain program's by a relative error of at most 0.025.
Values may be sent and summed in bfloat16 or wider, within the bound.
A program may use at most 128 MiB of HBM per device.

v0:
```python
import jax
import jax.numpy as jnp
from jax import lax
from jax.sharding import PartitionSpec as P

NSEG = 8


def product_nt(lhs_mat, rhs_mat):
    return lax.dot_general(
        lhs_mat, rhs_mat, (((1,), (1,)), ((), ())), preferred_element_type=jnp.float32
    )


def product_tn(lhs_mat, rhs_mat):
    return lax.dot_general(
        lhs_mat, rhs_mat, (((0,), (0,)), ((), ())), preferred_element_type=jnp.float32
    )


def shards(grad_out, grad_side, attn_out, gate_pre, up_pre, seg_ids, down_weight, out_weight):
    row_count = grad_out.shape[0]
    row_start = (lax.axis_index("gx") * lax.axis_size("gy") + lax.axis_index("gy")) * row_count
    onehot = (seg_ids[:, None] == jnp.arange(NSEG, dtype=jnp.int32)[None, :]).astype(jnp.float32)
    counts = jnp.sum(onehot, axis=0)
    own_rows = lax.dynamic_slice_in_dim(onehot, row_start, row_count, 0)
    length = own_rows @ counts
    tok_weight = seg_ids.shape[0] / (NSEG * length)
    grad_scaled = (tok_weight[:, None] * grad_out.astype(jnp.float32)).astype(jnp.bfloat16)
    grad_resid = (grad_scaled.astype(jnp.float32) + grad_side.astype(jnp.float32)).astype(
        jnp.bfloat16
    )
    gate_full = gate_pre.astype(jnp.float32)
    up_full = up_pre.astype(jnp.float32)
    sigmoid_gate = jax.nn.sigmoid(gate_full)
    hidden = (gate_full * sigmoid_gate * up_full).astype(jnp.bfloat16)
    hidden_rows, attn_rows = (
        lax.all_gather(hidden, "gz", axis=0, tiled=True),
        lax.all_gather(attn_out, "gz", axis=0, tiled=True),
    )
    scaled_rows, resid_rows = (
        lax.all_gather(grad_scaled, "gy", axis=0, tiled=True),
        lax.all_gather(grad_resid, "gy", axis=0, tiled=True),
    )
    down_rows, outw_rows = (
        lax.all_gather(down_weight, "gx", axis=0, tiled=True),
        lax.all_gather(out_weight, "gx", axis=0, tiled=True),
    )
    hidden_part = product_nt(scaled_rows, down_rows)
    attn_part = product_nt(resid_rows, outw_rows)
    down_part = product_tn(hidden_rows, scaled_rows)
    outw_part = product_tn(attn_rows, resid_rows)
    grad_down, grad_outproj = (
        lax.psum_scatter(
            down_part.astype(jnp.bfloat16), "gx", scatter_dimension=0, tiled=True
        ).astype(jnp.float32),
        lax.psum_scatter(
            outw_part.astype(jnp.bfloat16), "gx", scatter_dimension=0, tiled=True
        ).astype(jnp.float32),
    )
    grad_hidden, grad_attn = (
        lax.psum_scatter(
            hidden_part.astype(jnp.bfloat16), "gz", scatter_dimension=0, tiled=True
        ).astype(jnp.float32),
        lax.psum_scatter(
            attn_part.astype(jnp.bfloat16), "gz", scatter_dimension=0, tiled=True
        ).astype(jnp.float32),
    )
    grad_gate = (
        grad_hidden * up_full * sigmoid_gate * (1.0 + gate_full * (1.0 - sigmoid_gate))
    ).astype(jnp.bfloat16)
    grad_up = (grad_hidden * gate_full * sigmoid_gate).astype(jnp.bfloat16)
    return (
        grad_gate,
        grad_up,
        grad_attn.astype(jnp.bfloat16),
        grad_down.astype(jnp.bfloat16),
        grad_outproj.astype(jnp.bfloat16),
    )


def solution(mesh):
    return jax.shard_map(
        shards,
        mesh=mesh,
        in_specs=(
            P(("gx", "gy"), "gz"),
            P(("gx", "gy"), "gz"),
            P(("gx", "gz"), "gy"),
            P(("gx", "gz"), "gy"),
            P(("gx", "gz"), "gy"),
            P(),
            P(("gy", "gx"), "gz"),
            P(("gy", "gx"), "gz"),
        ),
        out_specs=(
            P(("gx", "gz"), "gy"),
            P(("gx", "gz"), "gy"),
            P(("gx", "gz"), "gy"),
            P(("gy", "gx"), "gz"),
            P(("gy", "gx"), "gz"),
        ),
        check_vma=False,
    )
```

profile of v0, /device:TPU:1, one launch (start us, length us, event | category | flops | bytes accessed | tf_op | source)
XLA Modules:
  0.0 556.8 jit_solution(7143069462041939692)
XLA Ops:
  7.2 0.0 all-gather.6.cloned.1.call-start
  7.2 0.7 iota_compare_fusion
  7.9 0.8 convert_reduce_fusion
  8.7 0.2 fusion.1
  8.9 1.8 add_convert_fusion
  10.7 0.0 all-gather.8.cloned.1.call-start
  10.8 0.7 all-gather.8.cloned.1.call-update
  11.5 0.0 reduce-scatter.5.cloned.1.call-start
  11.5 36.8 %all-gather.6.cloned.1.call-done = bf16[256,2048]{1,0:T(8,128)(2,1)} async-done(((bf16[32,2048]{1,0:T(8,128)(2,1)}), bf16[256,2048]{1,0:T(8,128)(2,1)}) %all-gather.6.cloned.1.call-update) | async-done | bytes 1048592 | tf_op jit(solution)/shard_map/all_gather | solution.py:42
  48.3 100.5 %all-gather.8.cloned.1.call-done = bf16[3328,2048]{1,0:T(8,128)(2,1)} async-done(((bf16[832,2048]{1,0:T(8,128)(2,1)}), bf16[3328,2048]{1,0:T(8,128)(2,1)}) %all-gather.8.cloned.1.call-update) | async-done | bytes 13631504 | tf_op jit(solution)/shard_map/all_gather | solution.py:46
  148.8 10.1 %convolution_convert_fusion.1 = bf16[256,3328]{1,0:T(8,128)(2,1)} fusion(bf16[256,2048]{1,0:T(8,128)(2,1)} %all-gather.6.cloned.1.call-done, bf16[3328,2048]{1,0:T(8,128)(2,1)} %all-gather.8.cloned.1.call-done), kind=kOutput, calls=%fused_computation.1 | convolution fusion | flops 3490512896 | bytes 16384000 | tf_op jit(solution)/shard_map/dot_general | solution.py:10
  159.0 0.0 all-gather.10.cloned.1.call-start
  159.0 0.5 all-gather.10.cloned.1.call-update
  159.5 0.0 all-gather.12.cloned.1.call-start
  159.6 0.5 all-gather.12.cloned.1.call-update
  160.1 0.0 all-gather.14.cloned.1.call-start
  160.2 36.5 %reduce-scatter.5.cloned.1.call-done = bf16[32,3328]{1,0:T(8,128)(2,1)} async-done(((bf16[256,3328]{1,0:T(8,128)(2,1)}), bf16[32,3328]{1,0:T(8,128)(2,1)}) %reduce-scatter.5.cloned.1.call-update) | async-done | bytes 213008 | tf_op jit(solution)/shard_map/reduce_scatter | solution.py:62
  196.7 2.0 fusion.5
  198.7 0.0 reduce-scatter.11.cloned.1.call-start
  198.8 22.5 %all_gather.23 = bf16[256,1024]{1,0:T(8,128)(2,1)S(1)} all-gather(bf16[32,1024]{1,0:T(8,128)(2,1)S(1)} %copy-done.4), channel_id=1, replica_groups=mesh['gx'=4,'gy'=8,'gz'=8] {'gz'}, dimensions={0}, use_global_device_ids=true | all-gather | bytes 589824 | tf_op jit(solution)/shard_map/all_gather | solution.py:39
  221.3 15.1 %all-gather.10.cloned.1.call-done = bf16[256,2048]{1,0:T(8,128)(2,1)} async-done(((bf16[32,2048]{1,0:T(8,128)(2,1)}), bf16[256,2048]{1,0:T(8,128)(2,1)}) %all-gather.10.cloned.1.call-update) | async-done | bytes 1048592 | tf_op jit(solution)/shard_map/all_gather | solution.py:43
  236.3 4.5 convert_bitcast_fusion
  240.8 0.0 reduce-scatter.7.cloned.1.call-start
  240.9 42.3 %all-gather.12.cloned.1.call-done = bf16[1024,2048]{1,0:T(8,128)(2,1)} async-done(((bf16[256,2048]{1,0:T(8,128)(2,1)}), bf16[1024,2048]{1,0:T(8,128)(2,1)}) %all-gather.12.cloned.1.call-update) | async-done | bytes 4194320 | tf_op jit(solution)/shard_map/all_gather | solution.py:47
  283.2 4.3 convolution_convert_fusion.2
  287.5 0.0 reduce-scatter.9.cloned.1.call-start
  287.5 35.0 %all-gather.14.cloned.1.call-done = bf16[256,3328]{1,0:T(8,128)(2,1)} async-done(((bf16[32,3328]{1,0:T(8,128)(2,1)}), bf16[256,3328]{1,0:T(8,128)(2,1)}) %all-gather.14.cloned.1.call-update) | async-done | bytes 1703952 | tf_op jit(solution)/shard_map/all_gather | solution.py:38
  322.5 8.3 %convolution_convert_fusion = bf16[3328,2048]{1,0:T(8,128)(2,1)} fusion(bf16[256,3328]{1,0:T(8,128)(2,1)} %all-gather.14.cloned.1.call-done, bf16[256,2048]{1,0:T(8,128)(2,1)S(1)} %copy-done.1), kind=kOutput, calls=%fused_computation | convolution fusion | flops 3496476672 | bytes 16384000 | tf_op jit(solution)/shard_map/dot_general | solution.py:16
  330.9 56.0 %reduce-scatter.11.cloned.1.call-done = bf16[256,2048]{0,1:T(8,128)(2,1)} async-done(((bf16[1024,2048]{0,1:T(8,128)(2,1)}), bf16[256,2048]{0,1:T(8,128)(2,1)}) %reduce-scatter.11.cloned.1.call-update) | async-done | bytes 1048592 | tf_op jit(solution)/shard_map/reduce_scatter | solution.py:57
  386.8 2.3 copy.14
  389.1 35.5 %reduce-scatter.7.cloned.1.call-done = bf16[32,1024]{1,0:T(8,128)(2,1)} async-done(((bf16[256,1024]{1,0:T(8,128)(2,1)}), bf16[32,1024]{1,0:T(8,128)(2,1)}) %reduce-scatter.7.cloned.1.call-update) | async-done | bytes 65552 | tf_op jit(solution)/shard_map/reduce_scatter | solution.py:65
  424.6 125.6 %reduce-scatter.9.cloned.1.call-done = bf16[832,2048]{1,0:T(8,128)(2,1)} async-done(((bf16[3328,2048]{1,0:T(8,128)(2,1)}), bf16[832,2048]{1,0:T(8,128)(2,1)}) %reduce-scatter.9.cloned.1.call-update) | async-done | bytes 3407888 | tf_op jit(solution)/shard_map/reduce_scatter | solution.py:54
  (16 shorter events, 0.1 us)
Async XLA Ops:
  7.2 41.1 %all-gather.6.cloned.1.call-start = ((), (), s32[]{:S(2)}) async-start(), calls=%async_computation.4 | async-start | bytes 1179648 | tf_op jit(solution)/shard_map/all_gather | solution.py:42
  10.7 138.1 %all-gather.8.cloned.1.call-start = ((), (), s32[]{:S(2)}) async-start(), calls=%async_computation.5 | async-start | bytes 17039360 | tf_op jit(solution)/shard_map/all_gather | solution.py:46
  11.5 185.3 %copy-start.2 = (bf16[32,3328]{1,0:T(8,128)(2,1)S(1)}, bf16[32,3328]{1,0:T(8,128)(2,1)}, u32[]{:S(2)}) copy-start(bf16[32,3328]{1,0:T(8,128)(2,1)} %param.12) | copy-start | bytes 638980
  11.5 185.2 %copy-start.3 = (bf16[32,3328]{1,0:T(8,128)(2,1)S(1)}, bf16[32,3328]{1,0:T(8,128)(2,1)}, u32[]{:S(2)}) copy-start(bf16[32,3328]{1,0:T(8,128)(2,1)} %param.11) | copy-start | bytes 638980
  11.5 185.2 %reduce-scatter.5.cloned.1.call-start = ((), (), s32[]{:S(2)}) async-start(), calls=%async_computation.6 | async-start | bytes 1916928 | tf_op jit(solution)/shard_map/reduce_scatter | solution.py:62
  158.9 39.9 %copy-start.4 = (bf16[32,1024]{1,0:T(8,128)(2,1)S(1)}, bf16[32,1024]{1,0:T(8,128)(2,1)}, u32[]{:S(2)}) copy-start(bf16[32,1024]{1,0:T(8,128)(2,1)} %param.10) | copy-start | bytes 196612
  159.0 77.4 %all-gather.10.cloned.1.call-start = ((), (), s32[]{:S(2)}) async-start(), calls=%async_computation.7 | async-start | bytes 1179648 | tf_op jit(solution)/shard_map/all_gather | solution.py:43
  159.5 123.6 %all-gather.12.cloned.1.call-start = ((), (), s32[]{:S(2)}) async-start(), calls=%async_computation.8 | async-start | bytes 5242880 | tf_op jit(solution)/shard_map/all_gather | solution.py:47
  160.1 162.4 %all-gather.14.cloned.1.call-start = ((), (), s32[]{:S(2)}) async-start(), calls=%async_computation.10 | async-start | bytes 1916928 | tf_op jit(solution)/shard_map/all_gather | solution.py:38
  198.7 188.1 %reduce-scatter.11.cloned.1.call-start = ((), (), s32[]{:S(2)}) async-start(), calls=%async_computation.12 | async-start | bytes 5242880 | tf_op jit(solution)/shard_map/reduce_scatter | solution.py:57
  240.8 42.4 %copy-start = (bf16[256,2048]{1,0:T(8,128)(2,1)S(1)}, bf16[256,2048]{1,0:T(8,128)(2,1)}, u32[]{:S(2)}) copy-start(bf16[256,2048]{1,0:T(8,128)(2,1)} %all-gather.10.cloned.1.call-done) | copy-start | bytes 3145732
  240.8 81.7 %copy-start.1 = (bf16[256,2048]{1,0:T(8,128)(2,1)S(1)}, bf16[256,2048]{1,0:T(8,128)(2,1)}, u32[]{:S(2)}) copy-start(bf16[256,2048]{1,0:T(8,128)(2,1)} %all-gather.6.cloned.1.call-done) | copy-start | bytes 3145732
  240.8 183.8 %reduce-scatter.7.cloned.1.call-start = ((), (), s32[]{:S(2)}) async-start(), calls=%async_computation.9 | async-start | bytes 589824 | tf_op jit(solution)/shard_map/reduce_scatter | solution.py:65
  287.5 262.8 %reduce-scatter.9.cloned.1.call-start = ((), (), s32[]{:S(2)}) async-start(), calls=%async_computation.11 | async-start | bytes 17039360 | tf_op jit(solution)/shard_map/reduce_scatter | solution.py:54
Sparse Core Ops, SparseCore 0:
  10.8 37.4 all-gather.5
  50.1 98.6 all-gather.7
  159.1 37.5 reduce-scatter.4
  198.5 37.7 all-gather.9
  238.1 44.9 all-gather.11
  285.5 36.9 all-gather.13
  325.5 61.2 reduce-scatter.10
  389.9 34.6 reduce-scatter.6
  428.3 121.8 reduce-scatter.8
where the time goes:
time: 557 us
  waiting for transfers between devices  485 us (87%)
  matrix products  27.4 us (5%)
  blocking collectives  22.5 us (4%)
  between operations  13.9 us (2%)
    reduce_scatter x1, waiting for transfers between devices, shards(): lax.psum_scatter(down_part.astype(jnp.bfloat16), 'gx', scatter_dimension=...  126 us
    all_gather x1, waiting for transfers between devices, shards(): lax.all_gather(down_weight, 'gx', axis=0, tiled=True)  101 us
    reduce_scatter x1, waiting for transfers between devices, shards(): lax.psum_scatter(outw_part.astype(jnp.bfloat16), 'gx', scatter_dimension=...  56 us
    all_gather x1, waiting for transfers between devices, shards(): lax.all_gather(out_weight, 'gx', axis=0, tiled=True)  42.3 us
    all_gather x1, waiting for transfers between devices, shards(): lax.all_gather(grad_scaled, 'gy', axis=0, tiled=True)  36.8 us
    reduce_scatter x1, waiting for transfers between devices, shards(): lax.psum_scatter(hidden_part.astype(jnp.bfloat16), 'gz', scatter_dimensio...  36.5 us
    reduce_scatter x1, waiting for transfers between devices, shards(): lax.psum_scatter(attn_part.astype(jnp.bfloat16), 'gz', scatter_dimension=...  35.5 us
    all_gather x1, waiting for transfers between devices, shards(): lax.all_gather(hidden, 'gz', axis=0, tiled=True)  35 us
  transfers between devices with their start and end apart: 9, of which 9 were waited for; matrix products, arithmetic and copies ran while one was open for 4% of the time, Pallas kernels for 0%

commit v1 on v0

--- a/solution.py
+++ b/solution.py
@@ -34,38 +34,33 @@
     up_full = up_pre.astype(jnp.float32)
     sigmoid_gate = jax.nn.sigmoid(gate_full)
     hidden = (gate_full * sigmoid_gate * up_full).astype(jnp.bfloat16)
-    hidden_rows, attn_rows = (
-        lax.all_gather(hidden, "gz", axis=0, tiled=True),
-        lax.all_gather(attn_out, "gz", axis=0, tiled=True),
-    )
-    scaled_rows, resid_rows = (
-        lax.all_gather(grad_scaled, "gy", axis=0, tiled=True),
-        lax.all_gather(grad_resid, "gy", axis=0, tiled=True),
-    )
-    down_rows, outw_rows = (
-        lax.all_gather(down_weight, "gx", axis=0, tiled=True),
-        lax.all_gather(out_weight, "gx", axis=0, tiled=True),
-    )
-    hidden_part = product_nt(scaled_rows, down_rows)
-    attn_part = product_nt(resid_rows, outw_rows)
-    down_part = product_tn(hidden_rows, scaled_rows)
-    outw_part = product_tn(attn_rows, resid_rows)
-    grad_down, grad_outproj = (
-        lax.psum_scatter(
-            down_part.astype(jnp.bfloat16), "gx", scatter_dimension=0, tiled=True
-        ).astype(jnp.float32),
-        lax.psum_scatter(
-            outw_part.astype(jnp.bfloat16), "gx", scatter_dimension=0, tiled=True
-        ).astype(jnp.float32),
-    )
-    grad_hidden, grad_attn = (
-        lax.psum_scatter(
-            hidden_part.astype(jnp.bfloat16), "gz", scatter_dimension=0, tiled=True
-        ).astype(jnp.float32),
-        lax.psum_scatter(
-            attn_part.astype(jnp.bfloat16), "gz", scatter_dimension=0, tiled=True
-        ).astype(jnp.float32),
-    )
+    row_blocks = lax.axis_size("gx")
+
+    def columns_in(part):
+        rows, cols = part.shape
+        spread = part.reshape(rows, row_blocks, cols // row_blocks)
+        spread = lax.all_to_all(spread, "gx", split_axis=1, concat_axis=0, tiled=True)
+        spread = spread.reshape(row_blocks, rows, cols // row_blocks)
+        spread = lax.all_gather(spread, "gz", axis=1, tiled=True)
+        return spread.reshape(-1, cols // row_blocks)
+
+    def columns_out(part):
+        rows, cols = part.shape
+        part = part.astype(jnp.bfloat16).reshape(row_blocks, rows // row_blocks, cols)
+        part = lax.psum_scatter(part, "gz", scatter_dimension=1, tiled=True)
+        part = lax.all_to_all(part, "gx", split_axis=0, concat_axis=2, tiled=True)
+        return part[0].astype(jnp.float32)
+
+    scaled_rows = lax.all_gather(grad_scaled, ("gx", "gy"), axis=0, tiled=True)
+    resid_rows = lax.all_gather(grad_resid, ("gx", "gy"), axis=0, tiled=True)
+    hidden_rows = columns_in(hidden)
+    attn_rows = columns_in(attn_out)
+    hidden_part = product_nt(scaled_rows, down_weight)
+    attn_part = product_nt(resid_rows, out_weight)
+    grad_down = product_tn(hidden_rows, scaled_rows)
+    grad_outproj = product_tn(attn_rows, resid_rows)
+    grad_hidden = columns_out(hidden_part)
+    grad_attn = columns_out(attn_part)
     grad_gate = (
         grad_hidden * up_full * sigmoid_gate * (1.0 + gate_full * (1.0 - sigmoid_gate))
     ).astype(jnp.bfloat16)

time: 557 us -> 399 us (0.72); the launches traced: 557 us -> 393 us
  waiting for transfers between devices: 485 us -> 258 us
  local copies, waits for them, and re-layouts: 2.29 us -> 30.1 us
  starting transfers between devices: 0.36 us -> 19.3 us
  blocking collectives: 22.5 us -> 40.5 us
    reduce_scatter x4 -> x1, waiting for transfers between devices: 254 us -> 0.01 us  [columns_out(): part = lax.psum_scatter(part, 'gz', scatter_dimension=1, tiled=True)]
    unnamed x9 -> x6, waiting for transfers between devices: 1.85 us -> 76.8 us
    all_gather x5 -> x3, waiting for transfers between devices: 230 us -> 180 us  [the longest x1 91.3 us: shards(): scaled_rows = lax.all_gather(grad_scaled, ('gx', 'gy'), axis=0, tiled=True)]
    all_to_all x0 -> x2, starting transfers between devices: none -> 19.1 us  [columns_out(): part = lax.all_to_all(part, 'gx', split_axis=0, concat_axis=2, tiled=True)]
    all_to_all x0 -> x2, blocking collectives: none -> 17.6 us  [columns_in(): lax.all_to_all(spread, 'gx', split_axis=1, concat_axis=0, tiled=True)]
    reshape x0 -> x5, local copies, waits for them, and re-layouts: none -> 12.5 us  [the longest x2 9.62 us: columns_out(): part.astype(jnp.bfloat16).reshape(row_blocks, rows // row_blocks, cols)]
    all_gather x0 -> x2, local copies, waits for them, and re-layouts: none -> 6.41 us  [columns_in(): spread = lax.all_gather(spread, 'gz', axis=1, tiled=True)]
  transfers between devices with their start and end apart: 9 -> 7, of which waited for: 9 -> 5; matrix products, arithmetic and copies ran while one was open for 4% -> 6% of each run, Pallas kernels for 0% -> 0%
where the time goes in v1:
time: 399 us; the launch traced here: 393 us
  waiting for transfers between devices  258 us (65%)
  blocking collectives  40.5 us (10%)
  local copies, waits for them, and re-layouts  30.1 us (8%)
  matrix products  23.7 us (6%)
  starting transfers between devices  19.3 us (5%)
  between operations  14.5 us (4%)
  other arithmetic  6.76 us (2%)
    all_gather x1, waiting for transfers between devices, shards(): scaled_rows = lax.all_gather(grad_scaled, ('gx', 'gy'), axis=0, tiled=True)  91.3 us
    all_gather x1, waiting for transfers between devices, shards(): resid_rows = lax.all_gather(grad_resid, ('gx', 'gy'), axis=0, tiled=True)  84.2 us
    unnamed x6, waiting for transfers between devices  76.8 us
    all_gather x1, blocking collectives, columns_in(): spread = lax.all_gather(spread, 'gz', axis=1, tiled=True)  22.9 us
    all_to_all x2, starting transfers between devices, columns_out(): part = lax.all_to_all(part, 'gx', split_axis=0, concat_axis=2, tiled=True)  19.1 us
    all_to_all x2, blocking collectives, columns_in(): lax.all_to_all(spread, 'gx', split_axis=1, concat_axis=0, tiled=True)  17.6 us
    dot_general x2, matrix products, product_tn(): lax.dot_general(lhs_mat, rhs_mat, (((0,), (0,)), ((), ())), preferred_ele...  11.9 us
    dot_general x2, matrix products, product_nt(): lax.dot_general(lhs_mat, rhs_mat, (((1,), (1,)), ((), ())), preferred_ele...  11.6 us
  transfers between devices with their start and end apart: 7, of which 5 were waited for; matrix products, arithmetic and copies ran while one was open for 6% of the time, Pallas kernels for 0%

profile of v1, /device:TPU:1, one launch (start us, length us, event | category | flops | bytes accessed | tf_op | source)
XLA Modules:
  0.0 392.9 jit_solution(7013000442510453469)
XLA Ops:
  7.2 0.8 iota_compare_fusion
  8.1 0.9 convert_reduce_fusion
  9.2 1.8 add_convert_fusion
  11.1 91.3 %all-gather.6.cloned.1.call-done = bf16[1024,2048]{1,0:T(8,128)(2,1)} async-done(((bf16[32,2048]{1,0:T(8,128)(2,1)}), bf16[1024,2048]{1,0:T(8,128)(2,1)}) %all-gather.6.cloned.1.call-update) | async-done | bytes 4194320 | tf_op jit(solution)/shard_map/all_gather | solution.py:54
  102.3 7.0 %convolution_convert_fusion.2 = bf16[1024,832]{0,1:T(8,128)(2,1)} fusion(bf16[1024,2048]{1,0:T(8,128)(2,1)} %all-gather.6.cloned.1.call-done, bf16[832,2048]{1,0:T(8,128)(2,1)S(1)} %copy-done), kind=kOutput, calls=%fused_computation.3 | convolution fusion | flops 3490512896 | bytes 9306112 | tf_op jit(solution)/shard_map/dot_general | solution.py:10
  109.4 4.3 %reshape.44 = bf16[4,256,832]{1,0,2:T(4,128)(2,1)} reshape(bf16[1024,832]{0,1:T(8,128)(2,1)} %convolution_convert_fusion.2) | data formatting | bytes 3407872 | tf_op jit(solution)/shard_map/reshape | solution.py:49
  113.7 5.3 %copy.45 = bf16[4,256,832]{2,0,1:T(4,128)(2,1)} copy(bf16[4,256,832]{1,0,2:T(4,128)(2,1)} %reshape.44) | data formatting | bytes 3407872 | tf_op jit(solution)/shard_map/reshape | solution.py:49
  121.0 76.1 %all-reduce.3.cloned.1.call-done = bf16[4,256,832]{2,0,1:T(4,128)(2,1)} async-done(((bf16[4,256,832]{2,0,1:T(4,128)(2,1)}), bf16[4,256,832]{2,0,1:T(4,128)(2,1)}) %all-reduce.3.cloned.1.call-update) | async-done | bytes 1703952
  197.1 1.0 constant_dynamic-slice_fusion
  198.1 0.7 copy.46
  198.8 8.9 %all-to-all-start = ((bf16[4,32,832]{2,1,0:T(8,128)(2,1)}), bf16[4,32,832]{2,1,0:T(8,128)(2,1)}, u32[]{:S(2)}, u32[]{:S(2)}) async-start(bf16[4,32,832]{2,1,0:T(8,128)(2,1)} %copy.46), calls=%async_computation | async-start | bytes 458752 | tf_op jit(solution)/shard_map/all_to_all | solution.py:51
  207.7 84.2 %all-gather.8.cloned.1.call-done = bf16[1024,2048]{1,0:T(8,128)(2,1)} async-done(((bf16[32,2048]{1,0:T(8,128)(2,1)}), bf16[1024,2048]{1,0:T(8,128)(2,1)}) %all-gather.8.cloned.1.call-update) | async-done | bytes 4194320 | tf_op jit(solution)/shard_map/all_gather | solution.py:55
  291.9 4.6 %convolution_convert_fusion.3 = bf16[1024,256]{1,0:T(8,128)(2,1)} fusion(bf16[1024,2048]{1,0:T(8,128)(2,1)} %all-gather.8.cloned.1.call-done, bf16[256,2048]{1,0:T(8,128)(2,1)} %param.15), kind=kOutput, calls=%fused_computation.4 | convolution fusion | flops 1074003968 | bytes 5767168 | tf_op jit(solution)/shard_map/dot_general | solution.py:10
  296.6 1.0 convert_bitcast_fusion
  297.6 1.1 copy.47
  298.6 2.1 reshape.52
  300.8 2.2 fusion.12
  303.0 1.9 reshape.46
  304.9 1.0 copy.49
  305.9 9.2 %all_to_all.54 = bf16[32,4,832]{2,0,1:T(8,128)(2,1)S(1)} all-to-all(bf16[32,4,832]{2,0,1:T(8,128)(2,1)S(1)} %copy.49), channel_id=1, replica_groups=mesh['gx'=4,'gy'=8,'gz'=8] {'gx'}, dimensions={1} | all-to-all | bytes 425984 | tf_op jit(solution)/shard_map/all_to_all | solution.py:42
  315.1 0.8 copy.50
  315.9 8.4 %all_to_all.55 = bf16[32,4,256]{2,0,1:T(8,128)(2,1)S(1)} all-to-all(bf16[32,4,256]{2,0,1:T(8,128)(2,1)S(1)} %bitcast.58), channel_id=1, replica_groups=mesh['gx'=4,'gy'=8,'gz'=8] {'gx'}, dimensions={1} | all-to-all | bytes 131072 | tf_op jit(solution)/shard_map/all_to_all | solution.py:42
  324.4 22.9 %all-gather.1 = bf16[4,256,1,256]{3,0,2,1:T(4,128)(2,1)S(1)} all-gather(bf16[4,32,1,256]{3,0,2,1:T(4,128)(2,1)S(1)} %copy.53), channel_id=3, replica_groups=mesh['gx'=4,'gy'=8,'gz'=8] {'gz'}, dimensions={1}, use_global_device_ids=true | all-gather | bytes 589824 | tf_op jit(solution)/shard_map/all_gather | solution.py:44
  347.2 0.9 copy.54
  348.1 10.2 %all-to-all-start.1 = ((bf16[4,32,256]{2,1,0:T(8,128)(2,1)}), bf16[4,32,256]{2,1,0:T(8,128)(2,1)S(1)}, u32[]{:S(2)}, u32[]{:S(2)}) async-start(bf16[4,32,256]{2,1,0:T(8,128)(2,1)} %reduce-scatter.2.cloned.1.call-done), calls=%async_computation.2 | async-start | bytes 131072 | tf_op jit(solution)/shard_map/all_to_all | solution.py:51
  358.4 4.6 %fusion = bf16[256,2048]{0,1:T(8,128)(2,1)} fusion(bf16[1024,2048]{1,0:T(8,128)(2,1)} %all-gather.8.cloned.1.call-done, bf16[1024,256]{1,0:T(8,128)(2,1)} %bitcast.54), kind=kOutput, calls=%fused_computation.2 | convolution fusion | flops 1074266112 | bytes 5767168 | tf_op jit(solution)/shard_map/dot_general | solution.py:16
  363.0 2.3 copy.55
  365.2 0.9 all-to-all-done.1
  366.8 4.9 %all-gather.10.cloned.1.call-done = bf16[4,256,1,832]{3,0,2,1:T(4,128)(2,1)} async-done(((bf16[4,32,1,832]{3,0,2,1:T(4,128)(2,1)}), bf16[4,256,1,832]{3,0,2,1:T(4,128)(2,1)}) %all-gather.10.cloned.1.call-update) | async-done | bytes 1703952 | tf_op jit(solution)/shard_map/all_gather | solution.py:44
  371.7 5.5 %copy.51 = bf16[4,256,1,832]{1,0,3,2:T(4,128)(2,1)} copy(bf16[4,256,1,832]{3,0,2,1:T(4,128)(2,1)} %all-gather.10.cloned.1.call-done) | data formatting | bytes 3407872 | tf_op jit(solution)/shard_map/all_gather | solution.py:44
  377.3 1.8 copy.58
  379.1 7.3 %convolution_convert_fusion = bf16[832,2048]{1,0:T(8,128)(2,1)} fusion(bf16[1024,832]{0,1:T(8,128)(2,1)S(1)} %bitcast.51, bf16[1024,2048]{1,0:T(8,128)(2,1)} %all-gather.6.cloned.1.call-done), kind=kOutput, calls=%fused_computation | convolution fusion | flops 3491364864 | bytes 9306112 | tf_op jit(solution)/shard_map/dot_general | solution.py:16
  (24 shorter events, 2.5 us)
Async XLA Ops:
  7.2 95.2 %copy-start = (bf16[832,2048]{1,0:T(8,128)(2,1)S(1)}, bf16[832,2048]{1,0:T(8,128)(2,1)}, u32[]{:S(2)}) copy-start(bf16[832,2048]{1,0:T(8,128)(2,1)} %param.14) | copy-start | bytes 10223620
  7.2 95.2 %all-gather.6.cloned.1.call-start = ((), (), s32[]{:S(2)}) async-start(), calls=%async_computation.5 | async-start | bytes 4325376 | tf_op jit(solution)/shard_map/all_gather | solution.py:54
  11.0 186.1 %all-reduce.3.cloned.1.call-start = ((), (), s32[]{:S(2)}) async-start(), calls=%async_computation.9 | async-start | bytes 3670016
  113.7 6.1 %copy-start.2 = (u32[256]{0:T(256)S(1)}, u32[256]{0:T(256)}, u32[]{:S(2)}) copy-start(u32[256]{0:T(256)} %constant.28) | copy-start | bytes 3076
  119.0 172.9 %all-gather.8.cloned.1.call-start = ((), (), s32[]{:S(2)}) async-start(), calls=%async_computation.6 | async-start | bytes 4325376 | tf_op jit(solution)/shard_map/all_gather | solution.py:55
  198.8 97.8 %all-to-all-start = ((bf16[4,32,832]{2,1,0:T(8,128)(2,1)}), bf16[4,32,832]{2,1,0:T(8,128)(2,1)}, u32[]{:S(2)}, u32[]{:S(2)}) async-start(bf16[4,32,832]{2,1,0:T(8,128)(2,1)} %copy.46), calls=%async_computation | async-start | bytes 458752 | tf_op jit(solution)/shard_map/all_to_all | solution.py:51
  207.7 140.4 %reduce-scatter.2.cloned.1.call-start = ((), (), s32[]{:S(2)}) async-start(), calls=%async_computation.7 | async-start | bytes 589824 | tf_op jit(solution)/shard_map/reduce_scatter | solution.py:50
  296.5 19.4 %copy-start.1 = (bf16[32,1024]{1,0:T(8,128)(2,1)S(1)}, bf16[32,1024]{1,0:T(8,128)(2,1)}, u32[]{:S(2)}) copy-start(bf16[32,1024]{1,0:T(8,128)(2,1)} %param.10) | copy-start | bytes 196612
  296.5 75.2 %all-gather.10.cloned.1.call-start = ((), (), s32[]{:S(2)}) async-start(), calls=%async_computation.8 | async-start | bytes 2064384 | tf_op jit(solution)/shard_map/all_gather | solution.py:44
  348.1 18.0 %all-to-all-start.1 = ((bf16[4,32,256]{2,1,0:T(8,128)(2,1)}), bf16[4,32,256]{2,1,0:T(8,128)(2,1)S(1)}, u32[]{:S(2)}, u32[]{:S(2)}) async-start(bf16[4,32,256]{2,1,0:T(8,128)(2,1)} %reduce-scatter.2.cloned.1.call-done), calls=%async_computation.2 | async-start | bytes 131072 | tf_op jit(solution)/shard_map/all_to_all | solution.py:51
Sparse Core Ops, SparseCore 0:
  11.3 90.9 all-gather.5
  119.1 77.9 all-reduce.2
  200.4 91.4 all-gather.7
  296.7 31.3 reduce-scatter.1
  329.9 41.8 all-gather.9

commit v2 on v1

v2 whole, which is shorter than its diff:
```python
import jax
import jax.numpy as jnp
from jax import lax
from jax.experimental import pallas as pl
from jax.experimental.pallas import tpu as pltpu
from jax.sharding import PartitionSpec as P

NSEG = 8
MESH = pl.DeviceIdType.MESH
F32, BF16 = jnp.float32, jnp.bfloat16

NZ, NX = 8, 4
ROWS = 32
WIDTH = 2048
FF, AT = 832, 256
COLS = AT + FF
TOKENS = 1024
TILE = 256


def product_nt(lhs_mat, rhs_mat):
    return lax.dot_general(lhs_mat, rhs_mat, (((1,), (1,)), ((), ())), preferred_element_type=F32)


def kernel(
    seg_ref, go_ref, gs_ref, attn_ref, gate_ref, up_ref, dw_hbm, ow_hbm,
    ggate_ref, gup_ref, gattn_ref, gdown_hbm, gout_hbm,
    dw, ow, grads, hsend, hid, hid_t, part, xin, yout, yin, dw_out, ow_out,
    w_sem, out_sem, zs, zr, ds, dr, ps, pr, h1s, h1r, h2s, h2r, c1s, c1r, c2s, c2r,
):
    gx, z, gz = lax.axis_index("gx"), lax.axis_index("gy"), lax.axis_index("gz")
    h, c, l, x = gx // 2, gx % 2, gz // NX, gz % NX

    def at(hh, cc, zz, ll, xx):
        return (hh * 2 + cc, zz, ll * NX + xx)

    def send(src, dst, send_sem, recv_sem, device):
        copy = pltpu.make_async_remote_copy(
            src_ref=src, dst_ref=dst, send_sem=send_sem, recv_sem=recv_sem,
            device_id=device, device_id_type=MESH,
        )
        copy.start()

    def sent(ref, sem):
        pltpu.make_async_copy(ref, ref, sem).wait()

    came = sent

    column = [(dh, dc, dl) for dh in range(2) for dc in range(2) for dl in range(2)][1:]

    def in_column(offset):
        dh, dc, dl = offset
        return (h + dh) % 2, (c + dc) % 2, (l + dl) % 2

    right, left = at(h, c, (z + 1) % NZ, l, x), at(h, c, (z + NZ - 1) % NZ, l, x)
    core = at(h, 1 - c, z, l, x)
    across = at(1 - h, c, z, l, x)
    x_right, x_left = at(h, c, z, l, (x + 1) % NX), at(h, c, z, l, (x + NX - 1) % NX)

    copy_dw = pltpu.make_async_copy(dw_hbm, dw, w_sem.at[0])
    copy_ow = pltpu.make_async_copy(ow_hbm, ow, w_sem.at[1])
    copy_dw.start()
    copy_ow.start()

    barrier = pltpu.get_barrier_semaphore()
    peers = [right, left]
    for offset in column:
        hh, cc, ll = in_column(offset)
        peers.append(at(hh, cc, z, ll, x))
    for dx in range(1, NX):
        peers.append(at(h, c, z, l, (x + dx) % NX))
    for peer in peers:
        pl.semaphore_signal(barrier, inc=1, device_id=peer, device_id_type=MESH)

    start = (gx * NZ + z) * ROWS
    seg = jnp.broadcast_to(seg_ref[...], (ROWS, TOKENS))
    token = lax.broadcasted_iota(jnp.int32, (ROWS, TOKENS), 1)
    row = lax.broadcasted_iota(jnp.int32, (ROWS, TOKENS), 0)
    own_id = jnp.sum(jnp.where(token == row + start, seg, 0), axis=1, keepdims=True)
    length = jnp.sum(jnp.where(seg == own_id, 1.0, 0.0).astype(F32), axis=1, keepdims=True)
    tok_weight = TOKENS / (NSEG * length)
    scaled = (tok_weight * go_ref[...].astype(F32)).astype(BF16)
    resid = (scaled.astype(F32) + gs_ref[...].astype(F32)).astype(BF16)
    grads[z, c, h, 0:ROWS] = scaled
    grads[z, c, h, ROWS:2 * ROWS] = resid

    pl.semaphore_wait(barrier, len(peers))

    def block(j, hh, cc=None):
        return grads.at[j, c if cc is None else cc, hh]

    def to_core(j, k, p):
        hh = h if p == 0 else 1 - h
        send(block(j, hh), block(j, hh), ds.at[k, p], dr.at[k, p], core)

    def to_z(direction, s, p, j):
        hh = h if p == 0 else 1 - h
        send(block(j, hh), block(j, hh), zs.at[direction, s, p], zr.at[direction, s, p],
             right if direction == 0 else left)

    send(block(z, h), block(z, h), ps, pr, across)
    to_z(0, 0, 0, z)
    to_z(1, 0, 0, z)
    to_core(z, 0, 0)

    gate = gate_ref[...].astype(F32)
    up = up_ref[...].astype(F32)
    hidden = (gate * jax.nn.sigmoid(gate) * up).astype(BF16)
    for g in range(4):
        hsend[g, :, AT:COLS] = hidden[:, g * FF:(g + 1) * FF]
        hsend[g, :, 0:AT] = attn_ref[:, g * AT:(g + 1) * AT]

    def hid_block(j, cc, hh):
        return hid.at[j, pl.ds(pl.multiple_of((cc * 2 + hh) * ROWS, ROWS), ROWS)]

    for o, offset in enumerate(column):
        hh, cc, ll = in_column(offset)
        send(hsend.at[hh * 2 + cc], hid_block(gz, c, h), h1s.at[o], h1r.at[o], at(hh, cc, z, ll, x))
    hid_block(gz, c, h)[...] = hsend[gx]

    came(block(z, 1 - h), pr)
    to_z(0, 0, 1, z)
    to_z(1, 0, 1, z)
    to_core(z, 0, 1)

    for o, offset in enumerate(column):
        hh, cc, ll = in_column(offset)
        came(hid_block(ll * NX + x, cc, hh), h1r.at[o])

    def chunk(ll, xx):
        return hid.at[ll * NX + xx]

    for i, ll in enumerate((0, 1)):
        send(chunk(ll, x), chunk(ll, x), h2s.at[0, i], h2r.at[0, i], x_right)
    for i, ll in enumerate((1, 0)):
        send(chunk(ll, x), chunk(ll, x), h2s.at[1, i], h2r.at[1, i], x_left)

    copy_dw.wait()
    copy_ow.wait()

    def product(j, k):
        scaled_rows = grads[j, :, :, 0:ROWS].reshape(4 * ROWS, WIDTH)
        resid_rows = grads[j, :, :, ROWS:2 * ROWS].reshape(4 * ROWS, WIDTH)
        part[j, :, AT:COLS] = product_nt(scaled_rows, dw[...]).astype(BF16)
        part[j, :, 0:AT] = product_nt(resid_rows, ow[...]).astype(BF16)
        dx = (j + NX - x) % NX

        @pl.when(dx != 0)
        def _():
            send(part.at[j], xin.at[j // NX, dx - 1], c1s.at[k], c1r.at[j // NX, dx - 1],
                 at(h, c, z, l, j % NX))

    def from_core(j, k, p):
        hh = h if p == 0 else 1 - h
        came(block(j, hh, 1 - c), dr.at[k, p])

    def from_z(direction, s, p, j):
        hh = h if p == 0 else 1 - h
        came(block(j, hh), zr.at[direction, s, p])

    for p in range(2):
        from_core(z, 0, p)
    product(z, 0)

    def relay_hidden():
        came(chunk(0, (x + 3) % NX), h2r.at[0, 0])
        send(chunk(0, (x + 3) % NX), chunk(0, (x + 3) % NX), h2s.at[0, 2], h2r.at[0, 2], x_right)
        came(chunk(1, (x + 1) % NX), h2r.at[1, 0])
        send(chunk(1, (x + 1) % NX), chunk(1, (x + 1) % NX), h2s.at[1, 2], h2r.at[1, 2], x_left)

    def pass_on(s, more):
        for p in range(2):
            for direction in range(2):
                j = (z + NZ - 1 - s) % NZ if direction == 0 else (z + 1 + s) % NZ
                k = 1 + 2 * s + direction
                from_z(direction, s, p, j)
                if more is None:
                    if p == direction:
                        to_z(direction, s + 1, p, j)
                else:
                    to_z(direction, s + 1, p, j)
                to_core(j, k, p)

    def products(s):
        def one(direction, carry):
            j = (z + NZ + (2 * direction - 1) * (1 + s)) % NZ
            k = 1 + 2 * s + direction
            for p in range(2):
                from_core(j, k, p)
            product(j, k)
            return carry

        lax.fori_loop(0, 2, one, 0)

    pass_on(0, True)
    relay_hidden()
    products(0)
    pass_on(1, True)
    products(1)
    pass_on(2, None)
    products(2)
    far = (z + 4) % NZ
    from_z(0, 3, 0, far)
    to_core(far, 7, 0)
    from_z(1, 3, 1, far)
    to_core(far, 7, 1)

    for i, (ll, xx) in enumerate(((0, 3), (1, 3), (0, 2))):
        if i:
            came(chunk(ll, (x + xx) % NX), h2r.at[0, i])
    for i, (ll, xx) in enumerate(((1, 1), (0, 1), (1, 2))):
        if i:
            came(chunk(ll, (x + xx) % NX), h2r.at[1, i])
    for j in range(NZ):
        hid_t[:, j * 4 * ROWS:(j + 1) * 4 * ROWS] = hid[j].T

    for p in range(2):
        from_core(far, 7, p)
    product(far, 7)

    def weight_grads(lo, hi):
        def one(t, carry):
            cols = pl.ds(pl.multiple_of(t * TILE, TILE), TILE)
            scaled_rows = grads[:, :, :, 0:ROWS, cols].reshape(TOKENS, TILE)
            dw_out[:, cols] = jnp.dot(
                hid_t[AT:COLS, :], scaled_rows, preferred_element_type=F32
            ).astype(BF16)
            resid_rows = grads[:, :, :, ROWS:2 * ROWS, cols].reshape(TOKENS, TILE)
            ow_out[:, cols] = jnp.dot(
                hid_t[0:AT, :], resid_rows, preferred_element_type=F32
            ).astype(BF16)
            return carry

        lax.fori_loop(lo, hi, one, 0)

    tiles = WIDTH // TILE
    weight_grads(0, tiles // 2)

    near = jnp.where((x + NZ - z) % NZ <= 2, 0, jnp.where((z + NZ - x) % NZ <= 2, 0, 1))

    def sum_x(ll, o_first):
        for dx in range(3):
            came(xin.at[ll, dx], c1r.at[ll, dx])
        total = part[ll * NX + x].astype(F32)
        for dx in range(3):
            total = total + xin[ll, dx].astype(F32)
        yout[ll] = total.astype(BF16)

    def yout_block(ll, cc, hh):
        return yout.at[ll, pl.ds(pl.multiple_of((cc * 2 + hh) * ROWS, ROWS), ROWS)]

    def send_y(dl):
        ll = (l + dl) % 2
        for o, offset in enumerate(column):
            if offset[2] == dl:
                hh, cc, _ = in_column(offset)
                send(yout_block(ll, cc, hh), yin.at[gx, l], c2s.at[o], c2r.at[o], at(hh, cc, z, ll, x))
        if dl == 0:
            yin[gx, l] = yout_block(l, c, h)[...]

    for dl in range(2):
        sum_x((l + dl) % 2, dl)
        send_y(dl)

    weight_grads(tiles // 2, tiles)
    copy_gd = pltpu.make_async_copy(dw_out, gdown_hbm, out_sem.at[0])
    copy_go = pltpu.make_async_copy(ow_out, gout_hbm, out_sem.at[1])
    copy_gd.start()
    copy_go.start()

    for o, offset in enumerate(column):
        hh, cc, ll = in_column(offset)
        came(yin.at[hh * 2 + cc, ll], c2r.at[o])
    summed = []
    for g in range(4):
        total = yin[g, 0].astype(F32) + yin[g, 1].astype(F32)
        gattn_ref[:, g * AT:(g + 1) * AT] = total[:, 0:AT].astype(BF16)
        summed.append(total[:, AT:COLS])
    grad_hidden = jnp.concatenate(summed, axis=1)
    gate = gate_ref[...].astype(F32)
    up = up_ref[...].astype(F32)
    sig = jax.nn.sigmoid(gate)
    ggate_ref[...] = (grad_hidden * up * sig * (1.0 + gate * (1.0 - sig))).astype(BF16)
    gup_ref[...] = (grad_hidden * gate * sig).astype(BF16)

    own = block(z, h)
    sent(own, ps)
    for s in range(4):
        for p in range(2):
            for direction in range(2):
                if s < 3 or p == direction:
                    sent(own, zs.at[direction, s, p])
    for k in range(8):
        for p in range(2):
            sent(own, ds.at[k, p])
    for o in range(7):
        sent(hsend.at[0], h1s.at[o])
        sent(yin.at[0, 0], c2s.at[o])
    for direction in range(2):
        for i in range(3):
            sent(hid.at[0], h2s.at[direction, i])
    for k in range(8):
        j = (z if k == 0 else (z + 4 if k == 7 else (z + NZ + (2 * ((k - 1) % 2) - 1) * (1 + (k - 1) // 2)))) % NZ

        @pl.when((j + NX - x) % NX != 0)
        def _():
            sent(part.at[0], c1s.at[k])

    copy_gd.wait()
    copy_go.wait()


def shards(grad_out, grad_side, attn_out, gate_pre, up_pre, seg_ids, down_weight, out_weight):
    vmem = pl.BlockSpec(memory_space=pltpu.VMEM)
    hbm = pl.BlockSpec(memory_space=pl.ANY)
    dma = pltpu.SemaphoreType.DMA
    return pl.pallas_call(
        kernel,
        out_shape=(
            jax.ShapeDtypeStruct(gate_pre.shape, BF16),
            jax.ShapeDtypeStruct(up_pre.shape, BF16),
            jax.ShapeDtypeStruct(attn_out.shape, BF16),
            jax.ShapeDtypeStruct(down_weight.shape, BF16),
            jax.ShapeDtypeStruct(out_weight.shape, BF16),
        ),
        in_specs=[vmem] * 6 + [hbm] * 2,
        out_specs=(vmem, vmem, vmem, hbm, hbm),
        scratch_shapes=[
            pltpu.VMEM((FF, WIDTH), BF16),
            pltpu.VMEM((AT, WIDTH), BF16),
            pltpu.VMEM((NZ, 2, 2, 2 * ROWS, WIDTH), BF16),
            pltpu.VMEM((4, ROWS, COLS), BF16),
            pltpu.VMEM((NZ, 4 * ROWS, COLS), BF16),
            pltpu.VMEM((COLS, TOKENS), BF16),
            pltpu.VMEM((NZ, 4 * ROWS, COLS), BF16),
            pltpu.VMEM((2, 3, 4 * ROWS, COLS), BF16),
            pltpu.VMEM((2, 4 * ROWS, COLS), BF16),
            pltpu.VMEM((4, 2, ROWS, COLS), BF16),
            pltpu.VMEM((FF, WIDTH), BF16),
            pltpu.VMEM((AT, WIDTH), BF16),
            dma((2,)),
            dma((2,)),
            dma((2, 4, 2)),
            dma((2, 4, 2)),
            dma((8, 2)),
            dma((8, 2)),
            dma,
            dma,
            dma((7,)),
            dma((7,)),
            dma((2, 3)),
            dma((2, 3)),
            dma((8,)),
            dma((2, 3)),
            dma((7,)),
            dma((7,)),
        ],
        compiler_params=pltpu.CompilerParams(
            collective_id=0, has_side_effects=True, vmem_limit_bytes=56 * 2**20
        ),
        cost_estimate=pl.CostEstimate(
            flops=4 * TOKENS * WIDTH * COLS, bytes_accessed=20 * 2**20, transcendentals=0
        ),
    )(
        seg_ids.reshape(1, TOKENS), grad_out, grad_side, attn_out, gate_pre, up_pre,
        down_weight, out_weight,
    )


def solution(mesh):
    return jax.shard_map(
        shards,
        mesh=mesh,
        in_specs=(
            P(("gx", "gy"), "gz"),
            P(("gx", "gy"), "gz"),
            P(("gx", "gz"), "gy"),
            P(("gx", "gz"), "gy"),
            P(("gx", "gz"), "gy"),
            P(),
            P(("gy", "gx"), "gz"),
            P(("gy", "gx"), "gz"),
        ),
        out_specs=(
            P(("gx", "gz"), "gy"),
            P(("gx", "gz"), "gy"),
            P(("gx", "gz"), "gy"),
            P(("gy", "gx"), "gz"),
            P(("gy", "gx"), "gz"),
        ),
        check_vma=False,
    )
```

time: 399 us -> 97.8 us (0.25); the launches traced: 393 us -> 97.6 us
  waiting for transfers between devices: 258 us -> 0 us
  Pallas kernels: 0 us -> 86.9 us
  blocking collectives: 40.5 us -> 0 us
  matrix products: 23.7 us -> 0 us
  local copies, waits for them, and re-layouts: 30.1 us -> 9.96 us
  starting transfers between devices: 19.3 us -> 0 us
  between operations: 14.5 us -> 0.65 us
  other arithmetic: 6.76 us -> 0 us
    all_gather x3 -> x0, waiting for transfers between devices: 180 us -> none  [the longest x1 91.3 us: shards(): scaled_rows = lax.all_gather(grad_scaled, ('gx', 'gy'), axis=0, tiled=True)]
    pallas_call x0 -> x1, Pallas kernels: none -> 86.9 us  [shards(): pl.pallas_call(kernel, out_shape=(jax.ShapeDtypeStruct(gate_pre.shape, BF...]
    unnamed x6 -> x0, waiting for transfers between devices: 76.8 us -> none
    dot_general x5 -> x0, matrix products: 23.7 us -> none  [the longest x2 11.9 us: product_tn(): lax.dot_general(lhs_mat, rhs_mat, (((0,), (0,)), ((), ())), preferred_ele...]
    all_gather x1 -> x0, blocking collectives: 22.9 us -> none  [columns_in(): spread = lax.all_gather(spread, 'gz', axis=1, tiled=True)]
    all_to_all x2 -> x0, starting transfers between devices: 19.1 us -> none  [columns_out(): part = lax.all_to_all(part, 'gx', split_axis=0, concat_axis=2, tiled=True)]
    all_to_all x2 -> x0, blocking collectives: 17.6 us -> none  [columns_in(): lax.all_to_all(spread, 'gx', split_axis=1, concat_axis=0, tiled=True)]
    reshape x5 -> x0, local copies, waits for them, and re-layouts: 12.5 us -> none  [the longest x2 9.62 us: columns_out(): part.astype(jnp.bfloat16).reshape(row_blocks, rows // row_blocks, cols)]
  transfers between devices with their start and end apart: 7 -> 0, of which waited for: 5 -> 0; matrix products, arithmetic and copies ran while one was open for 6% -> 0% of each run, Pallas kernels for 0% -> 0%
where the time goes in v2:
time: 97.8 us; the launch traced here: 97.6 us
  Pallas kernels  86.9 us (89%)
  local copies, waits for them, and re-layouts  9.96 us (10%)
    pallas_call x1, Pallas kernels, shards(): pl.pallas_call(kernel, out_shape=(jax.ShapeDtypeStruct(gate_pre.shape, BF...  86.9 us
    unnamed x7, local copies, waits for them, and re-layouts  9.96 us

profile of v2, /device:TPU:1, one launch (start us, length us, event | category | flops | bytes accessed | tf_op | source)
XLA Modules:
  0.0 97.6 jit_solution(540954197770830213)
XLA Ops:
  0.6 86.9 %shard_map.119 = (bf16[32,3328]{1,0:T(8,128)(2,1)}, bf16[32,3328]{1,0:T(8,128)(2,1)}, bf16[32,1024]{1,0:T(8,128)(2,1)}, bf16[832,2048]{1,0:T(8,128)(2,1)}, bf16[256,2048]{1,0:T(8,128)(2,1)}) custom-call(s32[1,1024]{1,0:T(1,128)} %bitcast.1, bf16[32,2048]{1,0:T(8,128)(2,1)} %go_ref.1, bf16[32,2048]{1,0:T(8,128)(2,1)} %gs_ref.1, bf16[32,1024]{1,0:T(8,128)(2,1)} %attn_ref.1, ...), custom_call_target="tpu_custom_call" | custom-call | flops 9126805504 | bytes 20971520 | tf_op jit(solution)/shard_map/pallas_call | solution.py:317
  87.6 1.6 %copy.18 = bf16[32,3328]{1,0:T(8,128)(2,1)} copy(bf16[32,3328]{1,0:T(8,128)(2,1)} %get-tuple-element.10) | data formatting | bytes 425984
  89.2 1.6 %copy.19 = bf16[32,3328]{1,0:T(8,128)(2,1)} copy(bf16[32,3328]{1,0:T(8,128)(2,1)} %get-tuple-element.11) | data formatting | bytes 425984
  90.8 1.5 %copy.20 = bf16[32,1024]{1,0:T(8,128)(2,1)} copy(bf16[32,1024]{1,0:T(8,128)(2,1)} %get-tuple-element.12) | data formatting | bytes 131072
  92.3 0.0 copy-start
  92.3 4.3 %copy.21 = bf16[832,2048]{1,0:T(8,128)(2,1)} copy(bf16[832,2048]{1,0:T(8,128)(2,1)} %get-tuple-element.13) | data formatting | bytes 6815744
  96.6 0.0 copy-done
  96.6 1.0 copy.22
Async XLA Ops:
  92.3 4.3 %copy-start = (bf16[256,2048]{1,0:T(8,128)(2,1)S(1)}, bf16[256,2048]{1,0:T(8,128)(2,1)}, u32[]{:S(2)}) copy-start(bf16[256,2048]{1,0:T(8,128)(2,1)} %get-tuple-element.14) | copy-start | bytes 3145732

commit v3 on v1

v3 whole, which is shorter than its diff:
```python
import jax
import jax.numpy as jnp
from jax import lax
from jax.experimental import pallas as pl
from jax.experimental.pallas import tpu as pltpu
from jax.sharding import PartitionSpec as P

NSEG = 8
MESH = pl.DeviceIdType.MESH
F32, BF16 = jnp.float32, jnp.bfloat16

NZ, NX = 8, 4
ROWS = 32
WIDTH = 2048
FF, AT = 832, 256
COLS = AT + FF
TOKENS = 1024
TILE = 256


def product_nt(lhs_mat, rhs_mat):
    return lax.dot_general(lhs_mat, rhs_mat, (((1,), (1,)), ((), ())), preferred_element_type=F32)


def kernel(
    seg_ref, go_ref, gs_ref, attn_ref, gate_ref, up_ref, dw_hbm, ow_hbm,
    ggate_ref, gup_ref, gattn_ref, dw_out, ow_out,
    dw, ow, grads, hsend, hx, hid, hid_t, part_f, part_a, xin_f, xin_a, yout_f, yout_a, yin_f, yin_a,
    w_sem, zs, zr, ds, dr, ps, pr, h1s, h1r, h2s, h2r, c1s, c1r, c2s, c2r,
):
    gx, z, gz = lax.axis_index("gx"), lax.axis_index("gy"), lax.axis_index("gz")
    h, c, l, x = gx // 2, gx % 2, gz // NX, gz % NX
    weights, part, xin = (dw, ow), (part_f, part_a), (xin_f, xin_a)
    yout, yin = (yout_f, yout_a), (yin_f, yin_a)

    def at(hh, cc, zz, ll, xx):
        return (hh * 2 + cc, zz, ll * NX + xx)

    def send(src, dst, send_sem, recv_sem, device):
        copy = pltpu.make_async_remote_copy(
            src_ref=src, dst_ref=dst, send_sem=send_sem, recv_sem=recv_sem,
            device_id=device, device_id_type=MESH,
        )
        copy.start()

    def sent(ref, sem):
        pltpu.make_async_copy(ref, ref, sem).wait()

    came = sent

    column = [(dh, dc, dl) for dh in range(2) for dc in range(2) for dl in range(2)][1:]

    def in_column(offset):
        dh, dc, dl = offset
        return (h + dh) % 2, (c + dc) % 2, (l + dl) % 2

    right, left = at(h, c, (z + 1) % NZ, l, x), at(h, c, (z + NZ - 1) % NZ, l, x)
    core = at(h, 1 - c, z, l, x)
    across = at(1 - h, c, z, l, x)

    copy_dw = pltpu.make_async_copy(dw_hbm, dw, w_sem.at[0])
    copy_ow = pltpu.make_async_copy(ow_hbm, ow, w_sem.at[1])
    copy_dw.start()
    copy_ow.start()

    barrier = pltpu.get_barrier_semaphore()
    peers = [right, left]
    for offset in column:
        hh, cc, ll = in_column(offset)
        peers.append(at(hh, cc, z, ll, x))
    for dx in range(1, NX):
        peers.append(at(h, c, z, l, (x + dx) % NX))
    for peer in peers:
        pl.semaphore_signal(barrier, inc=1, device_id=peer, device_id_type=MESH)

    def rows_of(ref, cc, hh):
        return ref.at[pl.ds(pl.multiple_of((cc * 2 + hh) * ROWS, ROWS), ROWS)]

    def block(q, j, hh, cc=None):
        return rows_of(grads.at[q, j], c if cc is None else cc, hh)

    start = (gx * NZ + z) * ROWS
    seg = jnp.broadcast_to(seg_ref[...], (ROWS, TOKENS))
    token = lax.broadcasted_iota(jnp.int32, (ROWS, TOKENS), 1)
    row = lax.broadcasted_iota(jnp.int32, (ROWS, TOKENS), 0)
    own_id = jnp.sum(jnp.where(token == row + start, seg, 0), axis=1, keepdims=True)
    length = jnp.sum(jnp.where(seg == own_id, 1.0, 0.0).astype(F32), axis=1, keepdims=True)
    tok_weight = TOKENS / (NSEG * length)
    scaled = (tok_weight * go_ref[...].astype(F32)).astype(BF16)
    block(0, z, h)[...] = scaled
    block(1, z, h)[...] = (scaled.astype(F32) + gs_ref[...].astype(F32)).astype(BF16)

    def to_core(q, j, k, p):
        hh = h if p == 0 else 1 - h
        send(block(q, j, hh), block(q, j, hh), ds.at[q, k, p], dr.at[q, k, p], core)

    def to_z(q, direction, s, p, j):
        hh = h if p == 0 else 1 - h
        send(block(q, j, hh), block(q, j, hh), zs.at[q, direction, s, p], zr.at[q, direction, s, p],
             right if direction == 0 else left)

    def from_core(q, j, k, p):
        hh = h if p == 0 else 1 - h
        came(block(q, j, hh, 1 - c), dr.at[q, k, p])

    def from_z(q, direction, s, p, j):
        hh = h if p == 0 else 1 - h
        came(block(q, j, hh), zr.at[q, direction, s, p])

    gate = gate_ref[...].astype(F32)
    up = up_ref[...].astype(F32)
    hidden = (gate * jax.nn.sigmoid(gate) * up).astype(BF16)
    for g in range(4):
        hsend[g, :, AT:COLS] = hidden[:, g * FF:(g + 1) * FF]
        hsend[g, :, 0:AT] = attn_ref[:, g * AT:(g + 1) * AT]

    pl.semaphore_wait(barrier, len(peers))

    def hid_block(ll, xx, cc, hh):
        return rows_of(hid.at[ll * NX + xx], cc, hh)

    def hidden_along_x():
        for dx in (1, 3, 2):
            send(hsend, hx.at[dx - 1], h1s.at[dx - 1], h1r.at[dx - 1], at(h, c, z, l, (x + NX - dx) % NX))

    def hidden_along_y(dx):
        source = hsend
        if dx:
            source = hx.at[dx - 1]
            came(source, h1r.at[dx - 1])
        xx = (x + dx) % NX
        for o, offset in enumerate(column):
            hh, cc, ll = in_column(offset)
            send(source.at[hh * 2 + cc], hid_block(l, xx, c, h), h2s.at[dx, o], h2r.at[dx, o],
                 at(hh, cc, z, ll, x))
        hid_block(l, xx, c, h)[...] = source[gx]

    def rest_of_hidden():
        for dx in range(NX):
            for o, offset in enumerate(column):
                hh, cc, ll = in_column(offset)
                came(hid_block(ll, (x + dx) % NX, cc, hh), h2r.at[dx, o])
        for j in range(NZ):
            hid_t[:, j * 4 * ROWS:(j + 1) * 4 * ROWS] = hid[j].T

    send(block(0, z, h), block(0, z, h), ps.at[0], pr.at[0], across)
    to_z(0, 0, 0, 0, z)
    to_z(0, 1, 0, 0, z)
    to_core(0, z, 0, 0)
    hidden_along_x()
    to_z(1, 0, 0, 0, z)
    to_z(1, 1, 0, 0, z)
    came(block(0, z, 1 - h), pr.at[0])
    to_z(0, 0, 0, 1, z)
    to_z(0, 1, 0, 1, z)
    to_core(0, z, 0, 1)
    send(block(1, z, h), block(1, z, h), ps.at[1], pr.at[1], across)
    hidden_along_y(0)

    def product(q, j, k):
        for p in range(2):
            from_core(q, j, k, p)
        part[q][j] = product_nt(grads[q, j], weights[q][...]).astype(BF16)
        dx = (j + NX - x) % NX

        @pl.when(dx != 0)
        def _():
            send(part[q].at[j], xin[q].at[j // NX, dx - 1], c1s.at[q, k], c1r.at[q, j // NX, dx - 1],
                 at(h, c, z, l, j % NX))

    def pass_on(q, s):
        for p in range(2):
            for direction in range(2):
                j = (z + NZ - 1 - s) % NZ if direction == 0 else (z + 1 + s) % NZ
                from_z(q, direction, s, p, j)
                if s < 2 or p == direction:
                    to_z(q, direction, s + 1, p, j)
                to_core(q, j, 1 + 2 * s + direction, p)

    def products(q, s):
        def one(direction, carry):
            product(q, (z + NZ + (2 * direction - 1) * (1 + s)) % NZ, 1 + 2 * s + direction)
            return carry

        lax.fori_loop(0, 2, one, 0)

    far = (z + 4) % NZ

    def pass_far(q):
        for p in range(2):
            from_z(q, p, 3, p, far)
            to_core(q, far, 7, p)

    def weight_grad(q, lo, hi):
        lhs, out = ((hid_t.at[AT:COLS], dw_out), (hid_t.at[0:AT], ow_out))[q]

        def one(t, carry):
            cols = pl.ds(pl.multiple_of(t * TILE, TILE), TILE)
            rows = grads[q, :, :, cols].reshape(TOKENS, TILE)
            out[:, cols] = jnp.dot(lhs[...], rows, preferred_element_type=F32).astype(BF16)
            return carry

        lax.fori_loop(lo, hi, one, 0)

    def sum_x(q, ll):
        for dx in range(3):
            came(xin[q].at[ll, dx], c1r.at[q, ll, dx])
        total = part[q][ll * NX + x].astype(F32)
        for dx in range(3):
            total = total + xin[q][ll, dx].astype(F32)
        yout[q][ll] = total.astype(BF16)

    def send_y(q, dl):
        ll = (l + dl) % 2
        for o, offset in enumerate(column):
            if offset[2] == dl:
                hh, cc, _ = in_column(offset)
                send(rows_of(yout[q].at[ll], cc, hh), yin[q].at[gx, l], c2s.at[q, o], c2r.at[q, o],
                     at(hh, cc, z, ll, x))
        if dl == 0:
            yin[q][gx, l] = rows_of(yout[q].at[l], c, h)[...]

    def summed(q):
        for o, offset in enumerate(column):
            hh, cc, ll = in_column(offset)
            came(yin[q].at[hh * 2 + cc, ll], c2r.at[q, o])
        return [yin[q][g, 0].astype(F32) + yin[q][g, 1].astype(F32) for g in range(4)]

    pass_on(0, 0)
    copy_dw.wait()
    copy_ow.wait()
    product(0, z, 0)
    pass_on(0, 1)
    hidden_along_y(1)
    hidden_along_y(3)
    products(0, 0)
    pass_on(0, 2)
    came(block(1, z, 1 - h), pr.at[1])
    to_z(1, 0, 0, 1, z)
    to_z(1, 1, 0, 1, z)
    to_core(1, z, 0, 0)
    to_core(1, z, 0, 1)
    hidden_along_y(2)
    products(0, 1)
    pass_far(0)
    products(0, 2)
    pass_on(1, 0)
    product(0, far, 7)
    product(1, z, 0)
    products(1, 0)
    pass_on(1, 1)
    rest_of_hidden()
    products(1, 1)
    weight_grad(0, 0, 3)
    pass_on(1, 2)
    products(1, 2)
    for dl in range(2):
        sum_x(0, (l + dl) % 2)
        send_y(0, dl)
    weight_grad(0, 3, 5)
    pass_far(1)
    product(1, far, 7)
    weight_grad(0, 5, 8)
    weight_grad(1, 0, 8)
    for dl in range(2):
        sum_x(1, (l + dl) % 2)
        send_y(1, dl)

    grad_hidden = jnp.concatenate(summed(0), axis=1)
    gate = gate_ref[...].astype(F32)
    up = up_ref[...].astype(F32)
    sig = jax.nn.sigmoid(gate)
    ggate_ref[...] = (grad_hidden * up * sig * (1.0 + gate * (1.0 - sig))).astype(BF16)
    gup_ref[...] = (grad_hidden * gate * sig).astype(BF16)
    gattn_ref[...] = jnp.concatenate(summed(1), axis=1).astype(BF16)

    own = block(0, z, h)
    for q in range(2):
        sent(own, ps.at[q])
        for s in range(4):
            for p in range(2):
                for direction in range(2):
                    if s < 3 or p == direction:
                        sent(own, zs.at[q, direction, s, p])
        for k in range(8):
            for p in range(2):
                sent(own, ds.at[q, k, p])
        for o in range(7):
            sent(yin[q].at[0, 0], c2s.at[q, o])
        for k in range(8):
            step, sign = (k + 1) // 2, 2 * ((k + 1) % 2) - 1
            j = (z + NZ + (sign * step if k else 0)) % NZ

            @pl.when((j + NX - x) % NX != 0)
            def _():
                sent(part[q].at[0], c1s.at[q, k])

    for dx in range(3):
        sent(hsend, h1s.at[dx])
    for dx in range(NX):
        for o in range(7):
            sent(hsend.at[0], h2s.at[dx, o])


PIECES = (1, 1, 1, 4, 2)


def copy_out(*refs):
    sources, results, sem = refs[:5], refs[5:10], refs[10]
    copies = []
    for source, result, pieces in zip(sources, results, PIECES):
        rows = source.shape[0] // pieces
        for i in range(pieces):
            part = pl.ds(i * rows, rows)
            copies.append(pltpu.make_async_copy(source.at[part], result.at[part], sem.at[len(copies)]))
    for copy in copies:
        copy.start()
    for copy in copies:
        copy.wait()


def shards(grad_out, grad_side, attn_out, gate_pre, up_pre, seg_ids, down_weight, out_weight):
    vmem = pl.BlockSpec(memory_space=pltpu.VMEM)
    hbm = pl.BlockSpec(memory_space=pl.ANY)
    dma = pltpu.SemaphoreType.DMA
    shapes = tuple(
        jax.ShapeDtypeStruct(like.shape, BF16)
        for like in (gate_pre, up_pre, attn_out, down_weight, out_weight)
    )
    results = pl.pallas_call(
        kernel,
        out_shape=tuple(pltpu.VMEM(like.shape, BF16) for like in shapes),
        in_specs=[vmem] * 6 + [pl.BlockSpec(memory_space=pltpu.HBM)] * 2,
        out_specs=(vmem,) * 5,
        scratch_shapes=[
            pltpu.VMEM((FF, WIDTH), BF16),
            pltpu.VMEM((AT, WIDTH), BF16),
            pltpu.VMEM((2, NZ, 4 * ROWS, WIDTH), BF16),
            pltpu.VMEM((4, ROWS, COLS), BF16),
            pltpu.VMEM((3, 4, ROWS, COLS), BF16),
            pltpu.VMEM((NZ, 4 * ROWS, COLS), BF16),
            pltpu.VMEM((COLS, TOKENS), BF16),
            pltpu.VMEM((NZ, 4 * ROWS, FF), BF16),
            pltpu.VMEM((NZ, 4 * ROWS, AT), BF16),
            pltpu.VMEM((2, 3, 4 * ROWS, FF), BF16),
            pltpu.VMEM((2, 3, 4 * ROWS, AT), BF16),
            pltpu.VMEM((2, 4 * ROWS, FF), BF16),
            pltpu.VMEM((2, 4 * ROWS, AT), BF16),
            pltpu.VMEM((4, 2, ROWS, FF), BF16),
            pltpu.VMEM((4, 2, ROWS, AT), BF16),
            dma((2,)),
            dma((2, 2, 4, 2)),
            dma((2, 2, 4, 2)),
            dma((2, 8, 2)),
            dma((2, 8, 2)),
            dma((2,)),
            dma((2,)),
            dma((3,)),
            dma((3,)),
            dma((4, 7)),
            dma((4, 7)),
            dma((2, 8)),
            dma((2, 2, 3)),
            dma((2, 7)),
            dma((2, 7)),
        ],
        compiler_params=pltpu.CompilerParams(
            collective_id=0, has_side_effects=True, vmem_limit_bytes=56 * 2**20
        ),
        cost_estimate=pl.CostEstimate(
            flops=4 * TOKENS * WIDTH * COLS, bytes_accessed=20 * 2**20, transcendentals=0
        ),
    )(
        seg_ids.reshape(1, TOKENS), grad_out, grad_side, attn_out, gate_pre, up_pre,
        down_weight, out_weight,
    )
    return pl.pallas_call(
        copy_out,
        out_shape=shapes,
        in_specs=[vmem] * 5,
        out_specs=(hbm,) * 5,
        scratch_shapes=[dma((sum(PIECES),))],
        compiler_params=pltpu.CompilerParams(vmem_limit_bytes=20 * 2**20),
    )(*results)


def solution(mesh):
    return jax.shard_map(
        shards,
        mesh=mesh,
        in_specs=(
            P(("gx", "gy"), "gz"),
            P(("gx", "gy"), "gz"),
            P(("gx", "gz"), "gy"),
            P(("gx", "gz"), "gy"),
            P(("gx", "gz"), "gy"),
            P(),
            P(("gy", "gx"), "gz"),
            P(("gy", "gx"), "gz"),
        ),
        out_specs=(
            P(("gx", "gz"), "gy"),
            P(("gx", "gz"), "gy"),
            P(("gx", "gz"), "gy"),
            P(("gy", "gx"), "gz"),
            P(("gy", "gx"), "gz"),
        ),
        check_vma=False,
    )
```

time: 399 us -> 74.4 us (0.19); the launches traced: 393 us -> 74.3 us
  waiting for transfers between devices: 258 us -> 0 us
  Pallas kernels: 0 us -> 73.7 us
  blocking collectives: 40.5 us -> 0 us
  local copies, waits for them, and re-layouts: 30.1 us -> 0 us
  matrix products: 23.7 us -> 0 us
  starting transfers between devices: 19.3 us -> 0 us
  between operations: 14.5 us -> 0.64 us
  other arithmetic: 6.76 us -> 0 us
    all_gather x3 -> x0, waiting for transfers between devices: 180 us -> none  [the longest x1 91.3 us: shards(): scaled_rows = lax.all_gather(grad_scaled, ('gx', 'gy'), axis=0, tiled=True)]
    unnamed x6 -> x0, waiting for transfers between devices: 76.8 us -> none
    pallas_call x0 -> x2, Pallas kernels: none -> 73.7 us  [the longest x1 71.3 us: shards(): pl.pallas_call(kernel, out_shape=tuple((pltpu.VMEM(like.shape, BF16) for...]
    dot_general x5 -> x0, matrix products: 23.7 us -> none  [the longest x2 11.9 us: product_tn(): lax.dot_general(lhs_mat, rhs_mat, (((0,), (0,)), ((), ())), preferred_ele...]
    all_gather x1 -> x0, blocking collectives: 22.9 us -> none  [columns_in(): spread = lax.all_gather(spread, 'gz', axis=1, tiled=True)]
    all_to_all x2 -> x0, starting transfers between devices: 19.1 us -> none  [columns_out(): part = lax.all_to_all(part, 'gx', split_axis=0, concat_axis=2, tiled=True)]
    all_to_all x2 -> x0, blocking collectives: 17.6 us -> none  [columns_in(): lax.all_to_all(spread, 'gx', split_axis=1, concat_axis=0, tiled=True)]
    reshape x5 -> x0, local copies, waits for them, and re-layouts: 12.5 us -> none  [the longest x2 9.62 us: columns_out(): part.astype(jnp.bfloat16).reshape(row_blocks, rows // row_blocks, cols)]
  transfers between devices with their start and end apart: 7 -> 0, of which waited for: 5 -> 0; matrix products, arithmetic and copies ran while one was open for 6% -> 0% of each run, Pallas kernels for 0% -> 0%
where the time goes in v3:
time: 74.4 us; the launch traced here: 74.3 us
  Pallas kernels  73.7 us (99%)
    pallas_call x1, Pallas kernels, shards(): pl.pallas_call(kernel, out_shape=tuple((pltpu.VMEM(like.shape, BF16) for...  71.3 us
    pallas_call x1, Pallas kernels, shards(): pl.pallas_call(copy_out, out_shape=shapes, in_specs=[vmem] * 5, out_specs...  2.33 us

profile of v3, /device:TPU:1, one launch (start us, length us, event | category | flops | bytes accessed | tf_op | source)
XLA Modules:
  0.0 74.3 jit_solution(17039457770977153740)
XLA Ops:
  0.6 71.3 %shard_map.119 = (bf16[32,3328]{1,0:T(8,128)(2,1)S(1)}, bf16[32,3328]{1,0:T(8,128)(2,1)S(1)}, bf16[32,1024]{1,0:T(8,128)(2,1)S(1)}, bf16[832,2048]{1,0:T(8,128)(2,1)S(1)}, bf16[256,2048]{1,0:T(8,128)(2,1)S(1)}) custom-call(s32[1,1024]{1,0:T(1,128)} %bitcast.1, bf16[32,2048]{1,0:T(8,128)(2,1)} %go_ref.1, bf16[32,2048]{1,0:T(8,128)(2,1)} %gs_ref.1, ...), custom_call_target="tpu_custom_call" | custom-call | flops 9126805504 | bytes 20971520 | tf_op jit(solution)/shard_map/pallas_call | solution.py:330
  72.0 2.3 %shard_map.120 = (bf16[32,3328]{1,0:T(8,128)(2,1)}, bf16[32,3328]{1,0:T(8,128)(2,1)}, bf16[32,1024]{1,0:T(8,128)(2,1)}, bf16[832,2048]{1,0:T(8,128)(2,1)}, bf16[256,2048]{1,0:T(8,128)(2,1)}) custom-call(bf16[32,3328]{1,0:T(8,128)(2,1)S(1)} %get-tuple-element.10.refs_0_, bf16[32,3328]{1,0:T(8,128)(2,1)S(1)} %get-tuple-element.11.refs_1_, ...), custom_call_target="tpu_custom_call" | custom-call | tf_op jit(solution)/shard_map/pallas_call | solution.py:377

commit v4 on v3

--- a/solution.py
+++ b/solution.py
@@ -23,9 +23,9 @@
 
 
 def kernel(
-    seg_ref, go_ref, gs_ref, attn_ref, gate_ref, up_ref, dw_hbm, ow_hbm,
+    seg_hbm, go_hbm, gs_hbm, attn_hbm, gate_hbm, up_hbm, dw_hbm, ow_hbm,
     ggate_ref, gup_ref, gattn_ref, dw_out, ow_out,
-    dw, ow, grads, hsend, hx, hid, hid_t, part_f, part_a, xin_f, xin_a, yout_f, yout_a, yin_f, yin_a,
+    seg_ref, go_ref, gs_ref, attn_ref, gate_ref, up_ref, dw, ow, grads, hsend, hx, hid, hid_t, part_f, part_a, xin_f, xin_a, yout_f, yout_a, yin_f, yin_a,
     w_sem, zs, zr, ds, dr, ps, pr, h1s, h1r, h2s, h2r, c1s, c1r, c2s, c2r,
 ):
     gx, z, gz = lax.axis_index("gx"), lax.axis_index("gy"), lax.axis_index("gz")
@@ -57,11 +57,6 @@
     right, left = at(h, c, (z + 1) % NZ, l, x), at(h, c, (z + NZ - 1) % NZ, l, x)
     core = at(h, 1 - c, z, l, x)
     across = at(1 - h, c, z, l, x)
-
-    copy_dw = pltpu.make_async_copy(dw_hbm, dw, w_sem.at[0])
-    copy_ow = pltpu.make_async_copy(ow_hbm, ow, w_sem.at[1])
-    copy_dw.start()
-    copy_ow.start()
 
     barrier = pltpu.get_barrier_semaphore()
     peers = [right, left]
@@ -73,12 +68,24 @@
     for peer in peers:
         pl.semaphore_signal(barrier, inc=1, device_id=peer, device_id_type=MESH)
 
+    fetches = [
+        pltpu.make_async_copy(source, target, w_sem.at[i])
+        for i, (source, target) in enumerate((
+            (seg_hbm, seg_ref), (go_hbm, go_ref), (gs_hbm, gs_ref), (gate_hbm, gate_ref),
+            (up_hbm, up_ref), (attn_hbm, attn_ref), (dw_hbm, dw), (ow_hbm, ow),
+        ))
+    ]
+    for fetch in fetches:
+        fetch.start()
+
     def rows_of(ref, cc, hh):
         return ref.at[pl.ds(pl.multiple_of((cc * 2 + hh) * ROWS, ROWS), ROWS)]
 
     def block(q, j, hh, cc=None):
         return rows_of(grads.at[q, j], c if cc is None else cc, hh)
 
+    for fetch in fetches[:3]:
+        fetch.wait()
     start = (gx * NZ + z) * ROWS
     seg = jnp.broadcast_to(seg_ref[...], (ROWS, TOKENS))
     token = lax.broadcasted_iota(jnp.int32, (ROWS, TOKENS), 1)
@@ -92,61 +99,66 @@
 
     def to_core(q, j, k, p):
         hh = h if p == 0 else 1 - h
-        send(block(q, j, hh), block(q, j, hh), ds.at[q, k, p], dr.at[q, k, p], core)
+        send(block(q, j, hh), block(q, j, hh), ds, dr.at[q, k], core)
 
     def to_z(q, direction, s, p, j):
         hh = h if p == 0 else 1 - h
-        send(block(q, j, hh), block(q, j, hh), zs.at[q, direction, s, p], zr.at[q, direction, s, p],
+        send(block(q, j, hh), block(q, j, hh), zs, zr.at[q, direction, s, p],
              right if direction == 0 else left)
 
-    def from_core(q, j, k, p):
-        hh = h if p == 0 else 1 - h
-        came(block(q, j, hh, 1 - c), dr.at[q, k, p])
+    def from_core(q, j, k):
+        came(grads.at[q, j, 0:2 * ROWS], dr.at[q, k])
 
     def from_z(q, direction, s, p, j):
         hh = h if p == 0 else 1 - h
         came(block(q, j, hh), zr.at[q, direction, s, p])
 
+    pl.semaphore_wait(barrier, len(peers))
+
+    def hid_block(ll, xx, cc, hh):
+        return rows_of(hid.at[ll * NX + xx], cc, hh)
+
+    def hidden_along_x():
+        for dx in (1, 3, 2):
+            send(hsend, hx.at[dx - 1], h1s, h1r.at[dx - 1], at(h, c, z, l, (x + NX - dx) % NX))
+
+    def hidden_along_y(dx):
+        source = hsend
+        if dx:
+            source = hx.at[dx - 1]
+            came(source, h1r.at[dx - 1])
+        xx = (x + dx) % NX
+        for offset in column:
+            if offset[0] <= offset[2]:
+                hh, cc, ll = in_column(offset)
+                send(source.at[hh * 2 + cc], hid_block(l, xx, c, h), h2s, h2r.at[dx, offset[0]],
+                     at(hh, cc, z, ll, x))
+        hid_block(l, xx, c, h)[...] = source[gx]
+
+    def relay_hidden(dx):
+        came(hid.at[0:2, 0:ROWS], h2r.at[dx, 1])
+        for cc in range(2):
+            rows = hid_block(1 - l, (x + dx) % NX, cc, 1 - h)
+            send(rows, rows, h2s, h2r.at[dx, 0], at(h, c, z, 1 - l, x))
+
+    def turn_hidden(dx):
+        came(hid.at[0:5, 0:ROWS], h2r.at[dx, 0])
+        for ll in range(2):
+            j = ll * NX + (x + dx) % NX
+            hid_t[:, pl.ds(pl.multiple_of(j * 4 * ROWS, 4 * ROWS), 4 * ROWS)] = hid[j].T
+
+    send(block(0, z, h), block(0, z, h), ps, pr.at[0], across)
+    to_z(0, 0, 0, 0, z)
+    to_z(0, 1, 0, 0, z)
+    to_core(0, z, 0, 0)
+    for fetch in fetches[3:6]:
+        fetch.wait()
     gate = gate_ref[...].astype(F32)
     up = up_ref[...].astype(F32)
     hidden = (gate * jax.nn.sigmoid(gate) * up).astype(BF16)
     for g in range(4):
         hsend[g, :, AT:COLS] = hidden[:, g * FF:(g + 1) * FF]
         hsend[g, :, 0:AT] = attn_ref[:, g * AT:(g + 1) * AT]
-
-    pl.semaphore_wait(barrier, len(peers))
-
-    def hid_block(ll, xx, cc, hh):
-        return rows_of(hid.at[ll * NX + xx], cc, hh)
-
-    def hidden_along_x():
-        for dx in (1, 3, 2):
-            send(hsend, hx.at[dx - 1], h1s.at[dx - 1], h1r.at[dx - 1], at(h, c, z, l, (x + NX - dx) % NX))
-
-    def hidden_along_y(dx):
-        source = hsend
-        if dx:
-            source = hx.at[dx - 1]
-            came(source, h1r.at[dx - 1])
-        xx = (x + dx) % NX
-        for o, offset in enumerate(column):
-            hh, cc, ll = in_column(offset)
-            send(source.at[hh * 2 + cc], hid_block(l, xx, c, h), h2s.at[dx, o], h2r.at[dx, o],
-                 at(hh, cc, z, ll, x))
-        hid_block(l, xx, c, h)[...] = source[gx]
-
-    def rest_of_hidden():
-        for dx in range(NX):
-            for o, offset in enumerate(column):
-                hh, cc, ll = in_column(offset)
-                came(hid_block(ll, (x + dx) % NX, cc, hh), h2r.at[dx, o])
-        for j in range(NZ):
-            hid_t[:, j * 4 * ROWS:(j + 1) * 4 * ROWS] = hid[j].T
-
-    send(block(0, z, h), block(0, z, h), ps.at[0], pr.at[0], across)
-    to_z(0, 0, 0, 0, z)
-    to_z(0, 1, 0, 0, z)
-    to_core(0, z, 0, 0)
     hidden_along_x()
     to_z(1, 0, 0, 0, z)
     to_z(1, 1, 0, 0, z)
@@ -154,28 +166,45 @@
     to_z(0, 0, 0, 1, z)
     to_z(0, 1, 0, 1, z)
     to_core(0, z, 0, 1)
-    send(block(1, z, h), block(1, z, h), ps.at[1], pr.at[1], across)
+    send(block(1, z, h), block(1, z, h), ps, pr.at[1], across)
     hidden_along_y(0)
 
     def product(q, j, k):
-        for p in range(2):
-            from_core(q, j, k, p)
+        from_core(q, j, k)
         part[q][j] = product_nt(grads[q, j], weights[q][...]).astype(BF16)
         dx = (j + NX - x) % NX
 
         @pl.when(dx != 0)
         def _():
-            send(part[q].at[j], xin[q].at[j // NX, dx - 1], c1s.at[q, k], c1r.at[q, j // NX, dx - 1],
+            send(part[q].at[j], xin[q].at[j // NX, dx - 1], c1s.at[q], c1r.at[q, j // NX],
                  at(h, c, z, l, j % NX))
+
+    def beyond(direction, s):
+        return (z + NZ - 1 - s) % NZ if direction == 0 else (z + 1 + s) % NZ
+
+    def cross_resid():
+        for direction in range(2):
+            j = beyond(direction, 0)
+            from_z(1, direction, 0, 0, j)
+            send(block(1, j, h), block(1, j, h), ps, pr.at[2 + direction], across)
+            to_core(1, j, 1 + direction, 0)
+
+    def pass_half(q, s, p):
+        for direction in range(2):
+            j = beyond(direction, s)
+            crossed = q == 1 and s == 0
+            if crossed and p == 1:
+                came(block(1, j, 1 - h), pr.at[2 + direction])
+            elif not crossed:
+                from_z(q, direction, s, p, j)
+            if s < 2 or p == direction:
+                to_z(q, direction, s + 1, p, j)
+            if not crossed or p == 1:
+                to_core(q, j, 1 + 2 * s + direction, p)
 
     def pass_on(q, s):
         for p in range(2):
-            for direction in range(2):
-                j = (z + NZ - 1 - s) % NZ if direction == 0 else (z + 1 + s) % NZ
-                from_z(q, direction, s, p, j)
-                if s < 2 or p == direction:
-                    to_z(q, direction, s + 1, p, j)
-                to_core(q, j, 1 + 2 * s + direction, p)
+            pass_half(q, s, p)
 
     def products(q, s):
         def one(direction, carry):
@@ -203,8 +232,7 @@
         lax.fori_loop(lo, hi, one, 0)
 
     def sum_x(q, ll):
-        for dx in range(3):
-            came(xin[q].at[ll, dx], c1r.at[q, ll, dx])
+        came(xin[q].at[ll], c1r.at[q, ll])
         total = part[q][ll * NX + x].astype(F32)
         for dx in range(3):
             total = total + xin[q][ll, dx].astype(F32)
@@ -215,56 +243,61 @@
         for o, offset in enumerate(column):
             if offset[2] == dl:
                 hh, cc, _ = in_column(offset)
-                send(rows_of(yout[q].at[ll], cc, hh), yin[q].at[gx, l], c2s.at[q, o], c2r.at[q, o],
+                send(rows_of(yout[q].at[ll], cc, hh), yin[q].at[gx * 2 + l], c2s.at[q], c2r.at[q],
                      at(hh, cc, z, ll, x))
         if dl == 0:
-            yin[q][gx, l] = rows_of(yout[q].at[l], c, h)[...]
+            yin[q][gx * 2 + l] = rows_of(yout[q].at[l], c, h)[...]
 
     def summed(q):
-        for o, offset in enumerate(column):
-            hh, cc, ll = in_column(offset)
-            came(yin[q].at[hh * 2 + cc, ll], c2r.at[q, o])
-        return [yin[q][g, 0].astype(F32) + yin[q][g, 1].astype(F32) for g in range(4)]
+        came(yin[q].at[0:7], c2r.at[q])
+        return [yin[q][2 * g].astype(F32) + yin[q][2 * g + 1].astype(F32) for g in range(4)]
 
     pass_on(0, 0)
-    copy_dw.wait()
-    copy_ow.wait()
+    for fetch in fetches[6:]:
+        fetch.wait()
+    cross_resid()
     product(0, z, 0)
     pass_on(0, 1)
+    relay_hidden(0)
     hidden_along_y(1)
     hidden_along_y(3)
     products(0, 0)
     pass_on(0, 2)
     came(block(1, z, 1 - h), pr.at[1])
-    to_z(1, 0, 0, 1, z)
-    to_z(1, 1, 0, 1, z)
     to_core(1, z, 0, 0)
     to_core(1, z, 0, 1)
+    pass_on(1, 0)
     hidden_along_y(2)
     products(0, 1)
     pass_far(0)
     products(0, 2)
-    pass_on(1, 0)
+    relay_hidden(1)
+    relay_hidden(3)
     product(0, far, 7)
     product(1, z, 0)
     products(1, 0)
     pass_on(1, 1)
-    rest_of_hidden()
     products(1, 1)
-    weight_grad(0, 0, 3)
-    pass_on(1, 2)
+    relay_hidden(2)
+    pass_half(1, 2, 0)
+    turn_hidden(0)
+    turn_hidden(1)
+    pass_half(1, 2, 1)
     products(1, 2)
+    turn_hidden(3)
+    turn_hidden(2)
     for dl in range(2):
         sum_x(0, (l + dl) % 2)
         send_y(0, dl)
-    weight_grad(0, 3, 5)
+    weight_grad(0, 0, 2)
     pass_far(1)
     product(1, far, 7)
-    weight_grad(0, 5, 8)
-    weight_grad(1, 0, 8)
+    weight_grad(0, 2, 7)
     for dl in range(2):
         sum_x(1, (l + dl) % 2)
         send_y(1, dl)
+    weight_grad(0, 7, 8)
+    weight_grad(1, 0, 8)
 
     grad_hidden = jnp.concatenate(summed(0), axis=1)
     gate = gate_ref[...].astype(F32)
@@ -274,32 +307,15 @@
     gup_ref[...] = (grad_hidden * gate * sig).astype(BF16)
     gattn_ref[...] = jnp.concatenate(summed(1), axis=1).astype(BF16)
 
-    own = block(0, z, h)
+    sent(grads.at[0, 0], ps)
+    sent(grads.at[0, 0:6], zs)
+    sent(grads.at[0, 0, 0:2 * ROWS], zs)
+    sent(grads.at[0], ds)
+    sent(hx, h1s)
+    sent(hid.at[0:7], h2s)
     for q in range(2):
-        sent(own, ps.at[q])
-        for s in range(4):
-            for p in range(2):
-                for direction in range(2):
-                    if s < 3 or p == direction:
-                        sent(own, zs.at[q, direction, s, p])
-        for k in range(8):
-            for p in range(2):
-                sent(own, ds.at[q, k, p])
-        for o in range(7):
-            sent(yin[q].at[0, 0], c2s.at[q, o])
-        for k in range(8):
-            step, sign = (k + 1) // 2, 2 * ((k + 1) % 2) - 1
-            j = (z + NZ + (sign * step if k else 0)) % NZ
-
-            @pl.when((j + NX - x) % NX != 0)
-            def _():
-                sent(part[q].at[0], c1s.at[q, k])
-
-    for dx in range(3):
-        sent(hsend, h1s.at[dx])
-    for dx in range(NX):
-        for o in range(7):
-            sent(hsend.at[0], h2s.at[dx, o])
+        sent(part[q].at[0:6], c1s.at[q])
+        sent(yin[q].at[0:7], c2s.at[q])
 
 
 PIECES = (1, 1, 1, 4, 2)
@@ -330,9 +346,15 @@
     results = pl.pallas_call(
         kernel,
         out_shape=tuple(pltpu.VMEM(like.shape, BF16) for like in shapes),
-        in_specs=[vmem] * 6 + [pl.BlockSpec(memory_space=pltpu.HBM)] * 2,
+        in_specs=[hbm] * 8,
         out_specs=(vmem,) * 5,
         scratch_shapes=[
+            pltpu.VMEM((1, TOKENS), jnp.int32),
+            pltpu.VMEM(grad_out.shape, BF16),
+            pltpu.VMEM(grad_side.shape, BF16),
+            pltpu.VMEM(attn_out.shape, BF16),
+            pltpu.VMEM(gate_pre.shape, BF16),
+            pltpu.VMEM(up_pre.shape, BF16),
             pltpu.VMEM((FF, WIDTH), BF16),
             pltpu.VMEM((AT, WIDTH), BF16),
             pltpu.VMEM((2, NZ, 4 * ROWS, WIDTH), BF16),
@@ -346,23 +368,23 @@
             pltpu.VMEM((2, 3, 4 * ROWS, AT), BF16),
             pltpu.VMEM((2, 4 * ROWS, FF), BF16),
             pltpu.VMEM((2, 4 * ROWS, AT), BF16),
-            pltpu.VMEM((4, 2, ROWS, FF), BF16),
-            pltpu.VMEM((4, 2, ROWS, AT), BF16),
+            pltpu.VMEM((8, ROWS, FF), BF16),
+            pltpu.VMEM((8, ROWS, AT), BF16),
+            dma((8,)),
+            dma,
+            dma((2, 2, 4, 2)),
+            dma,
+            dma((2, 8)),
+            dma,
+            dma((4,)),
+            dma,
+            dma((3,)),
+            dma,
+            dma((4, 2)),
             dma((2,)),
-            dma((2, 2, 4, 2)),
-            dma((2, 2, 4, 2)),
-            dma((2, 8, 2)),
-            dma((2, 8, 2)),
+            dma((2, 2)),
             dma((2,)),
             dma((2,)),
-            dma((3,)),
-            dma((3,)),
-            dma((4, 7)),
-            dma((4, 7)),
-            dma((2, 8)),
-            dma((2, 2, 3)),
-            dma((2, 7)),
-            dma((2, 7)),
         ],
         compiler_params=pltpu.CompilerParams(
             collective_id=0, has_side_effects=True, vmem_limit_bytes=56 * 2**20

time: 74.4 us -> 71.7 us (0.964)
  Pallas kernels: 73.7 us -> 70.9 us
    pallas_call x1, Pallas kernels: 71.3 us -> 68.6 us  [shards(): pl.pallas_call(kernel, out_shape=tuple((pltpu.VMEM(like.shape, BF16) for...]
where the time goes in v4:
time: 71.7 us; the launch traced here: 71.6 us
  Pallas kernels  70.9 us (99%)
    pallas_call x1, Pallas kernels, shards(): pl.pallas_call(kernel, out_shape=tuple((pltpu.VMEM(like.shape, BF16) for...  68.6 us
    pallas_call x1, Pallas kernels, shards(): pl.pallas_call(copy_out, out_shape=shapes, in_specs=[vmem] * 5, out_specs...  2.33 us

profile of v4, /device:TPU:1, one launch (start us, length us, event | category | flops | bytes accessed | tf_op | source)
XLA Modules:
  0.0 71.6 jit_solution(2873548235530898064)
XLA Ops:
  0.6 68.6 %shard_map.119 = (bf16[32,3328]{1,0:T(8,128)(2,1)S(1)}, bf16[32,3328]{1,0:T(8,128)(2,1)S(1)}, bf16[32,1024]{1,0:T(8,128)(2,1)S(1)}, bf16[832,2048]{1,0:T(8,128)(2,1)S(1)}, bf16[256,2048]{1,0:T(8,128)(2,1)S(1)}) custom-call(s32[1,1024]{1,0:T(1,128)} %bitcast.1, bf16[32,2048]{1,0:T(8,128)(2,1)} %go_hbm.1, bf16[32,2048]{1,0:T(8,128)(2,1)} %gs_hbm.1, ...), custom_call_target="tpu_custom_call" | custom-call | flops 9126805504 | bytes 20971520 | tf_op jit(solution)/shard_map/pallas_call | solution.py:346
  69.2 2.3 %shard_map.120 = (bf16[32,3328]{1,0:T(8,128)(2,1)}, bf16[32,3328]{1,0:T(8,128)(2,1)}, bf16[32,1024]{1,0:T(8,128)(2,1)}, bf16[832,2048]{1,0:T(8,128)(2,1)}, bf16[256,2048]{1,0:T(8,128)(2,1)}) custom-call(bf16[32,3328]{1,0:T(8,128)(2,1)S(1)} %get-tuple-element.10.refs_0_, bf16[32,3328]{1,0:T(8,128)(2,1)S(1)} %get-tuple-element.11.refs_1_, ...), custom_call_target="tpu_custom_call" | custom-call | tf_op jit(solution)/shard_map/pallas_call | solution.py:399

commit v5 on v4

--- a/solution.py
+++ b/solution.py
@@ -16,6 +16,7 @@
 COLS = AT + FF
 TOKENS = 1024
 TILE = 256
+TOP, BOTTOM = slice(0, 2 * ROWS), slice(2 * ROWS, 4 * ROWS)
 
 
 def product_nt(lhs_mat, rhs_mat):
@@ -25,8 +26,8 @@
 def kernel(
     seg_hbm, go_hbm, gs_hbm, attn_hbm, gate_hbm, up_hbm, dw_hbm, ow_hbm,
     ggate_ref, gup_ref, gattn_ref, dw_out, ow_out,
-    seg_ref, go_ref, gs_ref, attn_ref, gate_ref, up_ref, dw, ow, grads, hsend, hx, hid, hid_t, part_f, part_a, xin_f, xin_a, yout_f, yout_a, yin_f, yin_a,
-    w_sem, zs, zr, ds, dr, ps, pr, h1s, h1r, h2s, h2r, c1s, c1r, c2s, c2r,
+    seg_ref, go_ref, gs_ref, attn_ref, gate_ref, up_ref, dw, ow, grads, hsend, hx, hid, hid_t, part_f, part_a, mid, xin_f, xin_a, yout_f, yout_a, yin_f, yin_a,
+    w_sem, zs, zr, ds, dr, ps, pr, h1s, h1r, h2s, h2r, c1s, c1r, c1m, c2s, c2r,
 ):
     gx, z, gz = lax.axis_index("gx"), lax.axis_index("gy"), lax.axis_index("gz")
     h, c, l, x = gx // 2, gx % 2, gz // NX, gz % NX
@@ -57,6 +58,7 @@
     right, left = at(h, c, (z + 1) % NZ, l, x), at(h, c, (z + NZ - 1) % NZ, l, x)
     core = at(h, 1 - c, z, l, x)
     across = at(1 - h, c, z, l, x)
+    x_right, x_left = at(h, c, z, l, (x + 1) % NX), at(h, c, z, l, (x + NX - 1) % NX)
 
     barrier = pltpu.get_barrier_semaphore()
     peers = [right, left]
@@ -172,12 +174,51 @@
     def product(q, j, k):
         from_core(q, j, k)
         part[q][j] = product_nt(grads[q, j], weights[q][...]).astype(BF16)
+        part_on(q, j)
+
+    def part_on(q, j):
         dx = (j + NX - x) % NX
-
-        @pl.when(dx != 0)
+        ll = j // NX
+        if q == 1:
+
+            @pl.when(dx != 0)
+            def _():
+                send(part_a.at[j], xin_a.at[ll, dx - 1], c1s.at[1], c1r.at[1, ll], at(h, c, z, l, j % NX))
+
+            return
+
+        @pl.when(dx == 2)
         def _():
-            send(part[q].at[j], xin[q].at[j // NX, dx - 1], c1s.at[q], c1r.at[q, j // NX],
-                 at(h, c, z, l, j % NX))
+            send(part_f.at[j, TOP], mid.at[0, ll], c1s.at[0], c1m.at[0, ll], x_right)
+            send(part_f.at[j, BOTTOM], mid.at[1, ll], c1s.at[0], c1m.at[1, ll], x_left)
+
+        @pl.when(dx == 1)
+        def _():
+            send(part_f.at[j, BOTTOM], xin_f.at[ll, 0, BOTTOM], c1s.at[0], c1r.at[0, ll], x_right)
+
+        @pl.when(dx == 3)
+        def _():
+            send(part_f.at[j, TOP], xin_f.at[ll, 1, TOP], c1s.at[0], c1r.at[0, ll], x_left)
+
+    def add_on(j):
+        dx = (j + NX - x) % NX
+        ll = j // NX
+
+        def add(side, half, device):
+            came(mid.at[side, ll], c1m.at[side, ll])
+            total = part_f[j, half].astype(F32) + mid[side, ll].astype(F32)
+            part_f[j, half] = total.astype(BF16)
+            send(part_f.at[j, half], xin_f.at[ll, side, half], c1s.at[0], c1r.at[0, ll], device)
+
+        pl.when(dx == 1)(lambda: add(0, TOP, x_right))
+        pl.when(dx == 3)(lambda: add(1, BOTTOM, x_left))
+
+    def add_ons(s):
+        def one(direction, carry):
+            add_on((z + NZ + (2 * direction - 1) * (1 + s)) % NZ)
+            return carry
+
+        lax.fori_loop(0, 2, one, 0)
 
     def beyond(direction, s):
         return (z + NZ - 1 - s) % NZ if direction == 0 else (z + 1 + s) % NZ
@@ -207,8 +248,16 @@
             pass_half(q, s, p)
 
     def products(q, s):
+        js = [beyond(direction, s) for direction in range(2)]
+        for direction in range(2):
+            from_core(q, js[direction], 1 + 2 * s + direction)
+        both = jnp.concatenate([grads[q, j] for j in js], axis=0)
+        both = product_nt(both, weights[q][...]).astype(BF16)
+        for direction in range(2):
+            part[q][js[direction]] = both[direction * 4 * ROWS:(direction + 1) * 4 * ROWS]
+
         def one(direction, carry):
-            product(q, (z + NZ + (2 * direction - 1) * (1 + s)) % NZ, 1 + 2 * s + direction)
+            part_on(q, (z + NZ + (2 * direction - 1) * (1 + s)) % NZ)
             return carry
 
         lax.fori_loop(0, 2, one, 0)
@@ -234,19 +283,32 @@
     def sum_x(q, ll):
         came(xin[q].at[ll], c1r.at[q, ll])
         total = part[q][ll * NX + x].astype(F32)
-        for dx in range(3):
-            total = total + xin[q][ll, dx].astype(F32)
+        for i in range(xin[q].shape[1]):
+            total = total + xin[q][ll, i].astype(F32)
         yout[q][ll] = total.astype(BF16)
 
-    def send_y(q, dl):
-        ll = (l + dl) % 2
-        for o, offset in enumerate(column):
-            if offset[2] == dl:
-                hh, cc, _ = in_column(offset)
-                send(rows_of(yout[q].at[ll], cc, hh), yin[q].at[gx * 2 + l], c2s.at[q], c2r.at[q],
-                     at(hh, cc, z, ll, x))
-        if dl == 0:
-            yin[q][gx * 2 + l] = rows_of(yout[q].at[l], c, h)[...]
+    def send_y(q, ll):
+        for dh, dc in ((0, 0), (0, 1), (1, 0), (1, 1)):
+            hh, cc = (h + dh) % 2, (c + dc) % 2
+            rows = rows_of(yout[q].at[ll], cc, hh)
+
+            def away(rows=rows, hh=hh, cc=cc):
+                send(rows, yin[q].at[gx * 2 + l], c2s.at[q], c2r.at[q], at(hh, cc, z, ll, x))
+
+            if dh + dc:
+                away()
+            else:
+                pl.when(ll != l)(away)
+
+                @pl.when(ll == l)
+                def _():
+                    yin[q][gx * 2 + l] = rows[...]
+
+    near = (x + NZ + 2 - z) % NZ // 5
+
+    def sums_on(q, ll):
+        sum_x(q, ll)
+        send_y(q, ll)
 
     def summed(q):
         came(yin[q].at[0:7], c2r.at[q])
@@ -257,45 +319,51 @@
         fetch.wait()
     cross_resid()
     product(0, z, 0)
-    pass_on(0, 1)
+    pass_half(0, 1, 0)
+    products(0, 0)
+    pass_half(0, 1, 1)
     relay_hidden(0)
     hidden_along_y(1)
     hidden_along_y(3)
-    products(0, 0)
-    pass_on(0, 2)
+    add_on(z)
+    pass_half(0, 2, 0)
+    products(0, 1)
+    pass_half(0, 2, 1)
     came(block(1, z, 1 - h), pr.at[1])
     to_core(1, z, 0, 0)
     to_core(1, z, 0, 1)
     pass_on(1, 0)
     hidden_along_y(2)
-    products(0, 1)
+    add_ons(0)
+    products(0, 2)
     pass_far(0)
-    products(0, 2)
     relay_hidden(1)
     relay_hidden(3)
+    add_ons(1)
     product(0, far, 7)
     product(1, z, 0)
     products(1, 0)
-    pass_on(1, 1)
+    pass_half(1, 1, 0)
+    add_ons(2)
+    pass_half(1, 1, 1)
+    add_on(far)
     products(1, 1)
     relay_hidden(2)
     pass_half(1, 2, 0)
     turn_hidden(0)
     turn_hidden(1)
+    sums_on(0, near)
     pass_half(1, 2, 1)
     products(1, 2)
+    sums_on(0, 1 - near)
     turn_hidden(3)
     turn_hidden(2)
-    for dl in range(2):
-        sum_x(0, (l + dl) % 2)
-        send_y(0, dl)
+    sums_on(1, near)
     weight_grad(0, 0, 2)
     pass_far(1)
     product(1, far, 7)
     weight_grad(0, 2, 7)
-    for dl in range(2):
-        sum_x(1, (l + dl) % 2)
-        send_y(1, dl)
+    sums_on(1, 1 - near)
     weight_grad(0, 7, 8)
     weight_grad(1, 0, 8)
 
@@ -364,7 +432,8 @@
             pltpu.VMEM((COLS, TOKENS), BF16),
             pltpu.VMEM((NZ, 4 * ROWS, FF), BF16),
             pltpu.VMEM((NZ, 4 * ROWS, AT), BF16),
-            pltpu.VMEM((2, 3, 4 * ROWS, FF), BF16),
+            pltpu.VMEM((2, 2, 2 * ROWS, FF), BF16),
+            pltpu.VMEM((2, 2, 4 * ROWS, FF), BF16),
             pltpu.VMEM((2, 3, 4 * ROWS, AT), BF16),
             pltpu.VMEM((2, 4 * ROWS, FF), BF16),
             pltpu.VMEM((2, 4 * ROWS, AT), BF16),
@@ -382,6 +451,7 @@
             dma,
             dma((4, 2)),
             dma((2,)),
+            dma((2, 2)),
             dma((2, 2)),
             dma((2,)),
             dma((2,)),

time: 71.7 us -> 68.5 us (0.955)
  Pallas kernels: 70.9 us -> 67.8 us
    pallas_call x1, Pallas kernels: 68.6 us -> 65.5 us  [shards(): pl.pallas_call(kernel, out_shape=tuple((pltpu.VMEM(like.shape, BF16) for...]
where the time goes in v5:
time: 68.5 us; the launch traced here: 68.4 us
  Pallas kernels  67.8 us (99%)
    pallas_call x1, Pallas kernels, shards(): pl.pallas_call(kernel, out_shape=tuple((pltpu.VMEM(like.shape, BF16) for...  65.5 us
    pallas_call x1, Pallas kernels, shards(): pl.pallas_call(copy_out, out_shape=shapes, in_specs=[vmem] * 5, out_specs...  2.33 us

profile of v5, /device:TPU:1, one launch (start us, length us, event | category | flops | bytes accessed | tf_op | source)
XLA Modules:
  0.0 68.4 jit_solution(6180463781942934231)
XLA Ops:
  0.6 65.5 %shard_map.119 = (bf16[32,3328]{1,0:T(8,128)(2,1)S(1)}, bf16[32,3328]{1,0:T(8,128)(2,1)S(1)}, bf16[32,1024]{1,0:T(8,128)(2,1)S(1)}, bf16[832,2048]{1,0:T(8,128)(2,1)S(1)}, bf16[256,2048]{1,0:T(8,128)(2,1)S(1)}) custom-call(s32[1,1024]{1,0:T(1,128)} %bitcast.1, bf16[32,2048]{1,0:T(8,128)(2,1)} %go_hbm.1, bf16[32,2048]{1,0:T(8,128)(2,1)} %gs_hbm.1, ...), custom_call_target="tpu_custom_call" | custom-call | flops 9126805504 | bytes 20971520 | tf_op jit(solution)/shard_map/pallas_call | solution.py:414
  66.1 2.3 %shard_map.120 = (bf16[32,3328]{1,0:T(8,128)(2,1)}, bf16[32,3328]{1,0:T(8,128)(2,1)}, bf16[32,1024]{1,0:T(8,128)(2,1)}, bf16[832,2048]{1,0:T(8,128)(2,1)}, bf16[256,2048]{1,0:T(8,128)(2,1)}) custom-call(bf16[32,3328]{1,0:T(8,128)(2,1)S(1)} %get-tuple-element.10.refs_0_, bf16[32,3328]{1,0:T(8,128)(2,1)S(1)} %get-tuple-element.11.refs_1_, ...), custom_call_target="tpu_custom_call" | custom-call | tf_op jit(solution)/shard_map/pallas_call | solution.py:469

commit v6 on v5

--- a/solution.py
+++ b/solution.py
@@ -15,7 +15,7 @@
 FF, AT = 832, 256
 COLS = AT + FF
 TOKENS = 1024
-TILE = 256
+TILE = 512
 TOP, BOTTOM = slice(0, 2 * ROWS), slice(2 * ROWS, 4 * ROWS)
 
 
@@ -26,7 +26,7 @@
 def kernel(
     seg_hbm, go_hbm, gs_hbm, attn_hbm, gate_hbm, up_hbm, dw_hbm, ow_hbm,
     ggate_ref, gup_ref, gattn_ref, dw_out, ow_out,
-    seg_ref, go_ref, gs_ref, attn_ref, gate_ref, up_ref, dw, ow, grads, hsend, hx, hid, hid_t, part_f, part_a, mid, xin_f, xin_a, yout_f, yout_a, yin_f, yin_a,
+    seg_ref, go_ref, gs_ref, attn_ref, gate_ref, up_ref, gate_factor, up_factor, dw, ow, grads, hsend, hx, hid, hid_t, part_f, part_a, mid, xin_f, xin_a, yout_f, yout_a, yin_f, yin_a,
     w_sem, zs, zr, ds, dr, ps, pr, h1s, h1r, h2s, h2r, c1s, c1r, c1m, c2s, c2r,
 ):
     gx, z, gz = lax.axis_index("gx"), lax.axis_index("gy"), lax.axis_index("gz")
@@ -157,7 +157,11 @@
         fetch.wait()
     gate = gate_ref[...].astype(F32)
     up = up_ref[...].astype(F32)
-    hidden = (gate * jax.nn.sigmoid(gate) * up).astype(BF16)
+    sig = jax.nn.sigmoid(gate)
+    silu = gate * sig
+    hidden = (silu * up).astype(BF16)
+    up_factor[...] = silu
+    gate_factor[...] = up * sig * (1.0 + gate * (1.0 - sig))
     for g in range(4):
         hsend[g, :, AT:COLS] = hidden[:, g * FF:(g + 1) * FF]
         hsend[g, :, 0:AT] = attn_ref[:, g * AT:(g + 1) * AT]
@@ -345,34 +349,31 @@
     products(1, 0)
     pass_half(1, 1, 0)
     add_ons(2)
+    turn_hidden(0)
     pass_half(1, 1, 1)
     add_on(far)
     products(1, 1)
     relay_hidden(2)
+    turn_hidden(1)
     pass_half(1, 2, 0)
-    turn_hidden(0)
-    turn_hidden(1)
+    turn_hidden(3)
+    turn_hidden(2)
     sums_on(0, near)
+    weight_grad(0, 0, 1)
     pass_half(1, 2, 1)
     products(1, 2)
     sums_on(0, 1 - near)
-    turn_hidden(3)
-    turn_hidden(2)
     sums_on(1, near)
-    weight_grad(0, 0, 2)
+    weight_grad(0, 1, 2)
     pass_far(1)
     product(1, far, 7)
-    weight_grad(0, 2, 7)
+    weight_grad(0, 2, 4)
     sums_on(1, 1 - near)
-    weight_grad(0, 7, 8)
-    weight_grad(1, 0, 8)
+    weight_grad(1, 0, 4)
 
     grad_hidden = jnp.concatenate(summed(0), axis=1)
-    gate = gate_ref[...].astype(F32)
-    up = up_ref[...].astype(F32)
-    sig = jax.nn.sigmoid(gate)
-    ggate_ref[...] = (grad_hidden * up * sig * (1.0 + gate * (1.0 - sig))).astype(BF16)
-    gup_ref[...] = (grad_hidden * gate * sig).astype(BF16)
+    ggate_ref[...] = (grad_hidden * gate_factor[...]).astype(BF16)
+    gup_ref[...] = (grad_hidden * up_factor[...]).astype(BF16)
     gattn_ref[...] = jnp.concatenate(summed(1), axis=1).astype(BF16)
 
     sent(grads.at[0, 0], ps)
@@ -423,6 +424,8 @@
             pltpu.VMEM(attn_out.shape, BF16),
             pltpu.VMEM(gate_pre.shape, BF16),
             pltpu.VMEM(up_pre.shape, BF16),
+            pltpu.VMEM(gate_pre.shape, F32),
+            pltpu.VMEM(up_pre.shape, F32),
             pltpu.VMEM((FF, WIDTH), BF16),
             pltpu.VMEM((AT, WIDTH), BF16),
             pltpu.VMEM((2, NZ, 4 * ROWS, WIDTH), BF16),

time: 68.5 us -> 67.6 us (0.987)
  the two profiles are of different devices: /device:TPU:1 before, /device:TPU:9 now
where the time goes in v6:
time: 67.6 us; the launch traced here: 67.5 us
  Pallas kernels  66.9 us (99%)
    pallas_call x1, Pallas kernels, shards(): pl.pallas_call(kernel, out_shape=tuple((pltpu.VMEM(like.shape, BF16) for...  64.6 us
    pallas_call x1, Pallas kernels, shards(): pl.pallas_call(copy_out, out_shape=shapes, in_specs=[vmem] * 5, out_specs...  2.33 us

profile of v6, /device:TPU:9, one launch (start us, length us, event | category | flops | bytes accessed | tf_op | source)
XLA Modules:
  0.0 67.5 jit_solution(8097172865092746759)
XLA Ops:
  0.6 64.6 %shard_map.119 = (bf16[32,3328]{1,0:T(8,128)(2,1)S(1)}, bf16[32,3328]{1,0:T(8,128)(2,1)S(1)}, bf16[32,1024]{1,0:T(8,128)(2,1)S(1)}, bf16[832,2048]{1,0:T(8,128)(2,1)S(1)}, bf16[256,2048]{1,0:T(8,128)(2,1)S(1)}) custom-call(s32[1,1024]{1,0:T(1,128)} %bitcast.1, bf16[32,2048]{1,0:T(8,128)(2,1)} %go_hbm.1, bf16[32,2048]{1,0:T(8,128)(2,1)} %gs_hbm.1, ...), custom_call_target="tpu_custom_call" | custom-call | flops 9126805504 | bytes 20971520 | tf_op jit(solution)/shard_map/pallas_call | solution.py:415
  65.2 2.3 %shard_map.120 = (bf16[32,3328]{1,0:T(8,128)(2,1)}, bf16[32,3328]{1,0:T(8,128)(2,1)}, bf16[32,1024]{1,0:T(8,128)(2,1)}, bf16[832,2048]{1,0:T(8,128)(2,1)}, bf16[256,2048]{1,0:T(8,128)(2,1)}) custom-call(bf16[32,3328]{1,0:T(8,128)(2,1)S(1)} %get-tuple-element.10.refs_0_, bf16[32,3328]{1,0:T(8,128)(2,1)S(1)} %get-tuple-element.11.refs_1_, ...), custom_call_target="tpu_custom_call" | custom-call | tf_op jit(solution)/shard_map/pallas_call | solution.py:472
